TPU v7x, 256 devices: a whole 4x4x8 slice. The times are simulated.
256 devices in a mesh: rows: 16 (over y, x), cols: 16 (over z, core).
Axes of the slice: x: 4, y: 4, z: 8, core: 2. Of those that a mesh axis runs over, the one named last changes fastest.
Arguments:
- right_side: float32 [8, 512, 8192], P(None, 'rows', 'cols'), may hold values from -30 to 30
- east_class: int32 [512, 8192], P('rows', 'cols'), may hold values from 0 to 15
- lower_class: int32 [512, 8192], P('rows', 'cols'), may hold values from 0 to 15
- via_mask: int32 [512, 8192], P('rows', 'cols'), may hold values 0 or 1
- class_conductance: float32 [16], replicated, may hold values from 0.5 to 2
Outputs:
- solution_field: float32 [8, 512, 8192], P(None, 'rows', 'cols')
- residual: float32 [8, 512, 8192], P(None, 'rows', 'cols')
All inputs are finite; a program needn't handle non-finite values. No bound on the sum of `via_mask` on one device may be relied on, other than what follows from the above.
Results may differ from a plain program's by a relative error of at most 0.007.
Values sent between devices are 32-bit elements; how exact they have to be, the bound alone decides.
A program may use at most 64 MiB of HBM per device.

v0:
```python
import functools

import jax
import jax.numpy as jnp
from jax import lax
from jax.experimental import pallas as pl
from jax.experimental.pallas import tpu as pltpu
from jax.sharding import PartitionSpec as P

S = 5
OUTER = 2
D = S * OUTER
LEAK = 0.05
PAD_G = 2.0
SHIFT = 6.0
LANES = 128
CH = 16
MOMENTS = 14
SHIFTS = 5
f32 = jnp.float32
MESH = pl.DeviceIdType.MESH


def lane_bc(x, lane):
    return jnp.broadcast_to(x[:, lane : lane + 1], x.shape)


def row_bc(x, row):
    return jnp.broadcast_to(x[row : row + 1, :], x.shape)


def stencil_rows(src, dst, E, L, C, first, count):
    width = src.shape[-1]
    below = L[first - 1] * src[first - 1]
    for q in range(count):
        i = first + q
        v = src[i]
        e = E[i]
        l = L[i]
        dst[i] = (C[i] * v - e * pltpu.roll(v, width - 1, 1)) - (
            pltpu.roll(e * v, 1, 1) + (l * src[i + 1] + below)
        )
        below = l * v


def moments(V, first, rows, own):
    tiles = {}
    for s0, s1 in ((0, 3), (3, SHIFTS)):

        def row(i, acc):
            acc = list(acc)
            for t in range(own // LANES):
                sl = pl.ds(LANES * t, LANES)
                b = [V[m, i, :, sl] for m in range(S + 1)]
                w = [b[m] + b[m + 1] for m in range(S)]
                for s in range(s0, s1):
                    r = [b[m] if s == 0 else pltpu.roll(b[m], s, 0) for m in range(S)]
                    j = (s - s0) * MOMENTS
                    for k in range(2 * S - 1):
                        acc[j + k] = acc[j + k] + r[k // 2] * w[k - k // 2]
                    for k in range(S):
                        acc[j + 9 + k] = acc[j + 9 + k] + r[k // 2] * b[k - k // 2]
            return tuple(acc)

        zero = jnp.zeros((8, LANES), f32)
        acc = lax.fori_loop(first, first + rows, row, (zero,) * (MOMENTS * (s1 - s0)))
        for s in range(s0, s1):
            for k in range(MOMENTS):
                tiles[s, k] = acc[(s - s0) * MOMENTS + k]
    lane = lax.broadcasted_iota(jnp.int32, (8, LANES), 1)
    out = jnp.zeros((8, LANES), f32)
    for (s, k), x in tiles.items():
        total = jnp.broadcast_to(jnp.sum(x, axis=1, keepdims=True), x.shape)
        out = jnp.where(lane == s * MOMENTS + k, total, out)
    return out


def solve(packed):
    lane = lax.broadcasted_iota(jnp.int32, (8, LANES), 1)
    sub = lax.broadcasted_iota(jnp.int32, (8, LANES), 0)
    gap = (sub - lane) & 7
    full = []
    for k in range(MOMENTS):
        diag = [lane_bc(packed, s * MOMENTS + k) for s in range(SHIFTS)]
        x = diag[0]
        for s in range(1, SHIFTS):
            x = jnp.where(gap == s, diag[s], x)
        for s in range(1, 4):
            x = jnp.where(gap == 8 - s, pltpu.roll(diag[s], 8 - s, 0), x)
        full.append(x)
    block = lane >> 3
    T = []
    for m in range(S):
        x = full[9 + m] * (1.0 / SHIFT)
        for n in range(S):
            x = jnp.where(block == n, full[m + n], x)
        T.append(x)
    for kb in range(S):
        base = 8 * kb
        cols = {m: [lane_bc(T[m], base + j) for j in range(8)] for m in range(S)}
        piv = list(cols[kb])
        g = T[kb]
        for k in range(8):
            inv = 1.0 / row_bc(piv[k], k)
            here = sub == k
            for j in range(k + 1, 8):
                r = row_bc(piv[j], k) * inv
                piv[j] = jnp.where(here, r, piv[j] - piv[k] * r)
            r = row_bc(g, k) * inv
            g = jnp.where(here, r, g - piv[k] * r)
        q = [row_bc(g, a) for a in range(8)]
        for m in range(S):
            if m == kb:
                T[m] = g
                continue
            s0 = cols[m][0] * q[0]
            s1 = cols[m][1] * q[1]
            for a in range(2, 8, 2):
                s0 = s0 + cols[m][a] * q[a]
                s1 = s1 + cols[m][a + 1] * q[a + 1]
            T[m] = T[m] - (s0 + s1)
    return T


def spread(T, W):
    sub = lax.broadcasted_iota(jnp.int32, (8, LANES), 0)
    for m in range(S):
        cols = [lane_bc(T[m], 8 * S + k) for k in range(8)]
        for s in range(8):
            x = cols[0]
            for k in range(1, 8):
                x = jnp.where(((sub - s) & 7) == k, cols[k], x)
            W[8 * m + s] = x


def combine(V, W, X, first, rows, width):
    w = [W[j] for j in range(8 * S)]

    def row(i, c):
        for t in range(width // LANES):
            sl = pl.ds(LANES * t, LANES)
            b = [V[m, i, :, sl] for m in range(S)]
            out = None
            for s in range(8):
                z = b[0] * w[s]
                for m in range(1, S):
                    z = z + b[m] * w[8 * m + s]
                if s:
                    z = pltpu.roll(z, 8 - s, 0)
                out = z if out is None else out + z
            X[i, :, sl] = out
        return c

    lax.fori_loop(first, first + rows, row, 0)


def kernel(
    nr, nc, rhs, ecls, lcls, via, table, xo, ro,
    V, E, L, C, X1, X2, ELP, RE, RW, CE, CW, RB, W, hs, hr, rs, rr,
):
    rows, own = rhs.shape[1], rhs.shape[2]
    ext = rows + 2 * D
    width = own + LANES
    me_r = lax.axis_index("rows")
    me_c = lax.axis_index("cols")
    up, down = (me_r + nr - 1) % nr, (me_r + 1) % nr
    west, east = (me_c + nc - 1) % nc, (me_c + 1) % nc

    barrier = pltpu.get_barrier_semaphore()

    def greet(r, c):
        pl.semaphore_signal(barrier, inc=1, device_id=(r, c), device_id_type=MESH)

    for r in (up, down):
        for c in (west, east):
            greet(r, c)
    for d in range(1, nc):
        greet(me_r, (me_c + d) % nc)
    for d in range(1, nr):
        greet((me_r + d) % nr, me_c)

    for g in range(rows // 8):
        for t in range(own // LANES):
            rsl, sl = pl.ds(8 * g, 8), pl.ds(LANES * t, LANES)
            row_id = lax.broadcasted_iota(jnp.int32, (8, LANES), 0) + (me_r * rows + 8 * g)
            col_id = lax.broadcasted_iota(jnp.int32, (8, LANES), 1) + (me_c * own + LANES * t)
            ec, lc = ecls[rsl, sl], lcls[rsl, sl]
            e = jnp.zeros((8, LANES), f32)
            l = jnp.zeros((8, LANES), f32)
            for k in range(table.shape[0]):
                e = jnp.where(ec == k, table[k], e)
                l = jnp.where(lc == k, table[k], l)
            at = pl.ds(CH + 8 * g, 8)
            ELP[0, at, sl] = jnp.where(col_id < nc * own - 1, e, 0.0)
            ELP[1, at, sl] = jnp.where(row_id < nr * rows - 1, l, 0.0)
            ELP[2, at, sl] = PAD_G * via[rsl, sl].astype(f32)
            V[0, pl.ds(D + 8 * g, 8), :, sl] = jnp.swapaxes(rhs[:, rsl, sl], 0, 1)

    pl.semaphore_wait(barrier, nr + nc + 2)

    copies = []

    def send(src, dst, r, c):
        n = len(copies)
        copy = pltpu.make_async_remote_copy(
            src_ref=src, dst_ref=dst, send_sem=hs.at[n], recv_sem=hr.at[n],
            device_id=(r, c), device_id_type=MESH,
        )
        copy.start()
        copies.append(copy)

    top, bottom = pl.ds(D, D), pl.ds(rows, D)
    after, before = pl.ds(D + rows, D), pl.ds(0, D)
    inner = pl.ds(D, rows)
    body = pl.ds(0, own)
    lo, hi = pl.ds(0, LANES), pl.ds(own - LANES, LANES)
    send(V.at[0, top, :, body], V.at[0, after, :, body], up, me_c)
    send(V.at[0, bottom, :, body], V.at[0, before, :, body], down, me_c)
    send(V.at[0, inner, :, lo], RE.at[inner], me_r, west)
    send(V.at[0, inner, :, hi], RW.at[inner], me_r, east)
    send(V.at[0, top, :, lo], RE.at[after], up, west)
    send(V.at[0, bottom, :, lo], RE.at[before], down, west)
    send(V.at[0, top, :, hi], RW.at[after], up, east)
    send(V.at[0, bottom, :, hi], RW.at[before], down, east)
    ctop, cbottom = pl.ds(CH, CH), pl.ds(rows, CH)
    cafter, cbefore = pl.ds(CH + rows, CH), pl.ds(0, CH)
    cinner = pl.ds(CH, rows)
    send(ELP.at[:, ctop, body], ELP.at[:, cafter, body], up, me_c)
    send(ELP.at[:, cbottom, body], ELP.at[:, cbefore, body], down, me_c)
    send(ELP.at[:, cinner, lo], CE.at[:, cinner], me_r, west)
    send(ELP.at[:, cinner, hi], CW.at[:, cinner], me_r, east)
    send(ELP.at[:, ctop, lo], CE.at[:, cafter], up, west)
    send(ELP.at[:, cbottom, lo], CE.at[:, cbefore], down, west)
    send(ELP.at[:, ctop, hi], CW.at[:, cafter], up, east)
    send(ELP.at[:, cbottom, hi], CW.at[:, cbefore], down, east)
    for copy in copies:
        copy.wait_recv()
    for copy in copies:
        copy.wait_send()

    lane = lax.broadcasted_iota(jnp.int32, (8, LANES), 1)
    side = pl.ds(own, LANES)

    def side_row(i, c):
        V[0, i, :, side] = jnp.where(lane < LANES // 2, RE[i], RW[i])
        return c

    lax.fori_loop(0, ext, side_row, 0, unroll=4)
    crows = rows + 2 * CH
    for p in range(3):
        for g in range(crows // 8):
            at = pl.ds(8 * g, 8)
            ELP[p, at, side] = jnp.where(lane < LANES // 2, CE[p, at], CW[p, at])
    e, l = ELP[0], ELP[1]
    scale = 1.0 / SHIFT
    around = e + pltpu.roll(e, 1, 1) + l + pltpu.roll(l, 1, 0)
    ELP[2] = (around + (ELP[2] + LEAK)) * scale - 1.0
    ELP[0] = e * scale
    ELP[1] = l * scale

    def expand(i, c):
        for p, ref in enumerate((E, L, C)):
            ref[i] = jnp.broadcast_to(ELP[p, pl.ds(i + (CH - D), 1), :], (8, width))
        return c

    lax.fori_loop(0, ext, expand, 0, unroll=2)

    def allsum(phase, tile, me, n, device):
        RB[phase, me] = tile

        def put(d, c):
            pltpu.make_async_remote_copy(
                src_ref=RB.at[phase, me], dst_ref=RB.at[phase, me],
                send_sem=rs.at[phase], recv_sem=rr.at[phase],
                device_id=device((me + d) % n), device_id_type=MESH,
            ).start()
            return c

        lax.fori_loop(1, n, put, 0)
        pending(phase, n).wait_recv()
        parts = [RB[phase, d] for d in range(n)]
        while len(parts) > 1:
            odd = parts[len(parts) // 2 * 2 :]
            parts = [parts[j] + parts[j + 1] for j in range(0, len(parts) - 1, 2)] + odd
        return parts[0]

    def pending(phase, n):
        some = RB.at[phase, pl.ds(0, n - 1)]
        return pltpu.make_async_remote_copy(
            src_ref=some, dst_ref=some, send_sem=rs.at[phase], recv_sem=rr.at[phase],
            device_id=(up, me_c), device_id_type=MESH,
        )

    for sweep in range(OUTER):
        depth = S * (OUTER - sweep)
        a = D - depth + 1
        count = rows + 2 * depth - 2

        def level(m, c):
            stencil_rows(V.at[m], V.at[m + 1], E, L, C, a, count)
            return c

        lax.fori_loop(0, S, level, 0)
        tile = moments(V, D, rows, own)
        tile = allsum(2 * sweep, tile, me_c, nc, lambda c: (me_r, c))
        tile = allsum(2 * sweep + 1, tile, me_r, nr, lambda r: (r, me_c))
        spread(solve(tile), W)
        X = (X1, X2)[sweep]
        depth -= S
        combine(V, W, X, D - depth - 1, rows + 2 * depth + 2, width)
        stencil_rows(X, V.at[1], E, L, C, D - depth, rows + 2 * depth)

        def update(i, c):
            V[0, i] = V[0, i] - SHIFT * (V[1, i] + X[i])
            return c

        lax.fori_loop(D - depth, D + rows + depth, update, 0, unroll=2)

    for g in range(rows // 8):
        for t in range(own // LANES):
            rsl, sl = pl.ds(8 * g, 8), pl.ds(LANES * t, LANES)
            at = pl.ds(D + 8 * g, 8)
            xo[:, rsl, sl] = jnp.swapaxes(X1[at, :, sl] + X2[at, :, sl], 0, 1)
            ro[:, rsl, sl] = jnp.swapaxes(V[0, at, :, sl], 0, 1)
    for phase in range(2 * OUTER):
        pending(phase, (nc, nr)[phase % 2]).wait_send()


def local(right_side, east_class, lower_class, via_mask, class_conductance):
    nr, nc = lax.axis_size("rows"), lax.axis_size("cols")
    loads, rows, own = right_side.shape
    ext, width, crows = rows + 2 * D, own + LANES, rows + 2 * CH
    vmem = pl.BlockSpec(memory_space=pltpu.VMEM)
    field = pltpu.VMEM((ext, loads, width), f32)
    return pl.pallas_call(
        functools.partial(kernel, nr, nc),
        out_shape=[jax.ShapeDtypeStruct(right_side.shape, f32)] * 2,
        in_specs=[vmem] * 4 + [pl.BlockSpec(memory_space=pltpu.SMEM)],
        out_specs=[vmem] * 2,
        scratch_shapes=[
            pltpu.VMEM((S + 1, ext, loads, width), f32),
            field, field, field, field, field,
            pltpu.VMEM((3, crows, width), f32),
            pltpu.VMEM((ext, loads, LANES), f32),
            pltpu.VMEM((ext, loads, LANES), f32),
            pltpu.VMEM((3, crows, LANES), f32),
            pltpu.VMEM((3, crows, LANES), f32),
            pltpu.VMEM((2 * OUTER, max(nr, nc), 8, LANES), f32),
            pltpu.VMEM((8 * S, 8, LANES), f32),
            pltpu.SemaphoreType.DMA((16,)),
            pltpu.SemaphoreType.DMA((16,)),
            pltpu.SemaphoreType.DMA((2 * OUTER,)),
            pltpu.SemaphoreType.DMA((2 * OUTER,)),
        ],
        compiler_params=pltpu.CompilerParams(
            collective_id=0, has_side_effects=True, vmem_limit_bytes=40 * 2**20
        ),
    )(right_side, east_class, lower_class, via_mask, class_conductance)


def solution(mesh):
    return jax.shard_map(
        local,
        mesh=mesh,
        in_specs=(
            P(None, "rows", "cols"),
            P("rows", "cols"),
            P("rows", "cols"),
            P("rows", "cols"),
            P(),
        ),
        out_specs=(P(None, "rows", "cols"), P(None, "rows", "cols")),
        check_vma=False,
    )
```

profile of v0, /device:TPU:1, one launch (start us, length us, event | category | flops | bytes accessed | tf_op | source)
XLA Modules:
  0.0 72.2 jit_solution(14511502821377533871)
XLA Ops:
  0.6 0.0 copy-start
  0.6 1.0 %copy-done = f32[8,32,512]{2,1,0:T(8,128)S(1)} copy-done((f32[8,32,512]{2,1,0:T(8,128)S(1)}, f32[8,32,512]{2,1,0:T(8,128)}, u32[]{:S(2)}) %copy-start) | copy-done | bytes 524312
  1.7 0.0 copy-start.1
  1.7 0.8 %copy-done.1 = s32[32,512]{1,0:T(8,128)S(1)} copy-done((s32[32,512]{1,0:T(8,128)S(1)}, s32[32,512]{1,0:T(8,128)}, u32[]{:S(2)}) %copy-start.1) | copy-done | bytes 65560
  2.5 0.0 copy-start.2
  2.5 0.8 %copy-done.2 = s32[32,512]{1,0:T(8,128)S(1)} copy-done((s32[32,512]{1,0:T(8,128)S(1)}, s32[32,512]{1,0:T(8,128)}, u32[]{:S(2)}) %copy-start.2) | copy-done | bytes 65560
  3.4 0.0 copy-start.3
  3.4 0.8 %copy-done.3 = s32[32,512]{1,0:T(8,128)S(1)} copy-done((s32[32,512]{1,0:T(8,128)S(1)}, s32[32,512]{1,0:T(8,128)}, u32[]{:S(2)}) %copy-start.3) | copy-done | bytes 65560
  4.2 0.0 copy-start.4
  4.2 0.7 copy-done.4
  4.8 65.8 %shard_map.68 = (f32[8,32,512]{2,1,0:T(8,128)S(1)}, f32[8,32,512]{2,1,0:T(8,128)S(1)}) custom-call(f32[8,32,512]{2,1,0:T(8,128)S(1)} %copy-done, s32[32,512]{1,0:T(8,128)S(1)} %copy-done.1, s32[32,512]{1,0:T(8,128)S(1)} %copy-done.2, s32[32,512]{1,0:T(8,128)S(1)} %copy-done.3, f32[16]{0:T(128)S(1)} %copy-done.4), custom_call_target="tpu_custom_call" | custom-call | tf_op jit(solution)/shard_map/pallas_call | solution.py:335
  70.7 0.8 %copy.9 = f32[8,32,512]{2,1,0:T(8,128)} copy(f32[8,32,512]{2,1,0:T(8,128)S(1)} %get-tuple-element.4) | data formatting | bytes 1048576
  71.5 0.8 %copy.10 = f32[8,32,512]{2,1,0:T(8,128)} copy(f32[8,32,512]{2,1,0:T(8,128)S(1)} %get-tuple-element.5) | data formatting | bytes 1048576
Async XLA Ops:
  0.6 1.0 %copy-start = (f32[8,32,512]{2,1,0:T(8,128)S(1)}, f32[8,32,512]{2,1,0:T(8,128)}, u32[]{:S(2)}) copy-start(f32[8,32,512]{2,1,0:T(8,128)} %rhs.1) | copy-start | bytes 1572868
  1.7 0.8 %copy-start.1 = (s32[32,512]{1,0:T(8,128)S(1)}, s32[32,512]{1,0:T(8,128)}, u32[]{:S(2)}) copy-start(s32[32,512]{1,0:T(8,128)} %ecls.1) | copy-start | bytes 196612
  2.5 0.8 %copy-start.2 = (s32[32,512]{1,0:T(8,128)S(1)}, s32[32,512]{1,0:T(8,128)}, u32[]{:S(2)}) copy-start(s32[32,512]{1,0:T(8,128)} %lcls.1) | copy-start | bytes 196612
  3.4 0.8 %copy-start.3 = (s32[32,512]{1,0:T(8,128)S(1)}, s32[32,512]{1,0:T(8,128)}, u32[]{:S(2)}) copy-start(s32[32,512]{1,0:T(8,128)} %via.1) | copy-start | bytes 196612
  4.2 0.7 copy-start.4
where the time goes:
time: 72.5 us; the launch traced here: 72.2 us
  Pallas kernels  65.8 us (91%)
  local copies, waits for them, and re-layouts  5.79 us (8%)
    pallas_call x1, Pallas kernels, local(): pl.pallas_call(functools.partial(kernel, nr, nc), out_shape=[jax.ShapeDty...  65.8 us
    unnamed x12, local copies, waits for them, and re-layouts  5.79 us

commit v1 on v0

v1 whole, which is shorter than its diff:
```python
import functools

import jax
import jax.numpy as jnp
from jax import lax
from jax.experimental import pallas as pl
from jax.experimental.pallas import tpu as pltpu
from jax.sharding import PartitionSpec as P

S = 5
OUTER = 2
D = S * OUTER
LEAK = 0.05
PAD_G = 2.0
SHIFT = 6.0
LANES = 128
CH = 16
f32 = jnp.float32
bf16 = jnp.bfloat16
MESH = pl.DeviceIdType.MESH


def lane_bc(x, lane):
    return jnp.broadcast_to(x[:, lane : lane + 1], x.shape)


def row_bc(x, row):
    return jnp.broadcast_to(x[row : row + 1, :], x.shape)


def stencil_rows(src, E, L, C, first, count, put):
    width = src.shape[-1]
    below = L[first - 1] * src[first - 1]
    for q in range(count):
        i = first + q
        v = src[i]
        e = E[i]
        l = L[i]
        put(
            i,
            (C[i] * v - e * pltpu.roll(v, width - 1, 1))
            - (pltpu.roll(e * v, 1, 1) + (l * src[i + 1] + below)),
        )
        below = l * v


def halves(x):
    high = x.astype(bf16)
    low = (x - high.astype(f32)).astype(bf16)
    return jnp.concatenate([high, low], 0)


def moments(V, VB, first, rows, own, step=8):
    def some(j, acc):
        left, right = [], []
        for q in range(step):
            i = first + j * step + q
            b = [V[m, i] for m in range(S + 1)]
            split = halves(jnp.concatenate(b[:S], 0))
            VB[i] = split
            left.append(split[:, :own])
            right.append(
                halves(jnp.concatenate([(b[m] + b[m + 1])[:, :own] for m in range(S)] + [b[0][:, :own]], 0))
            )
        return acc + lax.dot_general(
            jnp.concatenate(left, 1), jnp.concatenate(right, 1),
            (((1,), (1,)), ((), ())), preferred_element_type=f32,
        )

    n, k = 8 * S, 8 * (S + 1)
    acc = lax.fori_loop(0, rows // step, some, jnp.zeros((2 * n, 2 * k), f32))
    gram = (acc[:n, :k] + acc[n:, k:]) + (acc[:n, k:] + acc[n:, :k])
    gram = jnp.concatenate([gram, jnp.zeros((n, LANES - k), f32)], 1)
    block = lax.broadcasted_iota(jnp.int32, (8, LANES), 1) >> 3
    out = jnp.zeros((8, LANES), f32)
    for m in range(S):
        x = gram[8 * m : 8 * m + 8]
        out = jnp.where((block >> 1) == m, x if m == 0 else pltpu.roll(x, 8 * m, 1), out)
    for m in range(S):
        x = pltpu.roll(gram[8 * m : 8 * m + 8], 32 + 8 * m, 1)
        out = jnp.where(block == 9 + m, x, out)
    return out


def solve(packed):
    lane = lax.broadcasted_iota(jnp.int32, (8, LANES), 1)
    sub = lax.broadcasted_iota(jnp.int32, (8, LANES), 0)
    T = [packed if m == 0 else pltpu.roll(packed, LANES - 8 * m, 1) for m in range(S)]
    T.append(pltpu.roll(packed, LANES - 72, 1) * (1.0 / SHIFT))
    for kb in range(S):
        base = 8 * kb
        cols = {m: [lane_bc(T[m], base + j) for j in range(8)] for m in range(kb, S + 1)}
        piv = list(cols[kb])
        within = (lane >= base) & (lane < base + 8)
        g = jnp.where(within, jnp.where(lane - base == sub, -1.0, 0.0), T[kb])
        for k in range(8):
            inv = 1.0 / row_bc(piv[k], k)
            here = sub == k
            for j in range(k + 1, 8):
                r = row_bc(piv[j], k) * inv
                piv[j] = jnp.where(here, r, piv[j] - piv[k] * r)
            r = row_bc(g, k) * inv
            g = jnp.where(here, r, g - piv[k] * r)
        q = [row_bc(g, a) for a in range(8)]
        for m in range(kb + 1, S + 1):
            s0 = cols[m][0] * q[0]
            s1 = cols[m][1] * q[1]
            for a in range(2, 8, 2):
                s0 = s0 + cols[m][a] * q[a]
                s1 = s1 + cols[m][a + 1] * q[a + 1]
            T[m] = jnp.where(within, 0.0, T[m]) - (s0 + s1)
    return T[S]


def combine(VB, coefficients, X, first, rows, step):
    lane = lax.broadcasted_iota(jnp.int32, (8, LANES), 1)
    n = 8 * S
    twice = jnp.where(lane < n, coefficients, pltpu.roll(coefficients, n, 1))
    left = halves(twice)[:, : 2 * n]

    def some(j, c):
        for q in range(step):
            i = first + j * step + q
            out = lax.dot_general(
                left, VB[i], (((1,), (0,)), ((), ())), preferred_element_type=f32
            )
            X[i] = out[:8] + out[8:]
        return c

    lax.fori_loop(0, rows // step, some, 0)


def kernel(
    nr, nc, rhs_in, ecls_in, lcls_in, via_in, table_in, xo, ro,
    rhs, ecls, lcls, via, table,
    V, VB, E, L, C, X1, X2, ELP, CP, RE, RW, CE, CW, CS, CR, RB, ls, hs, hr, rs, rr,
):
    rows, own = rhs.shape[1], rhs.shape[2]
    ext = rows + 2 * D
    width = own + LANES
    me_r = lax.axis_index("rows")
    me_c = lax.axis_index("cols")
    up, down = (me_r + nr - 1) % nr, (me_r + 1) % nr
    west, east = (me_c + nc - 1) % nc, (me_c + 1) % nc

    loads = []
    for j, (src, dst) in enumerate(
        ((rhs_in, rhs), (ecls_in, ecls), (lcls_in, lcls), (via_in, via), (table_in, table))
    ):
        loads.append(pltpu.make_async_copy(src, dst, ls.at[j]))
        loads[-1].start()

    barrier = pltpu.get_barrier_semaphore()

    def greet(r, c):
        pl.semaphore_signal(barrier, inc=1, device_id=(r, c), device_id_type=MESH)

    for r in (up, down):
        for c in (west, east):
            greet(r, c)
    for d in range(1, nc):
        greet(me_r, (me_c + d) % nc)
    for d in range(1, nr):
        greet((me_r + d) % nr, me_c)

    copies = [None] * 16

    def send(n, src, dst, r, c):
        copies[n] = pltpu.make_async_remote_copy(
            src_ref=src, dst_ref=dst, send_sem=hs.at[n], recv_sem=hr.at[n],
            device_id=(r, c), device_id_type=MESH,
        )
        copies[n].start()

    lane = lax.broadcasted_iota(jnp.int32, (8, LANES), 1)
    tiles = [(8 * g, LANES * t) for g in range(rows // 8) for t in range(own // LANES)]
    loads[0].wait()
    for r0, c0 in tiles:
        V[0, pl.ds(D + r0, 8), :, pl.ds(c0, LANES)] = jnp.swapaxes(
            rhs[:, pl.ds(r0, 8), pl.ds(c0, LANES)], 0, 1
        )

    pl.semaphore_wait(barrier, nr + nc + 2)

    body = pl.ds(0, own)
    lo, hi = pl.ds(0, LANES), pl.ds(own - LANES, LANES)
    inner = pl.ds(D, rows)
    send(0, V.at[0, pl.ds(D, S), :, body], V.at[0, pl.ds(D + rows, S), :, body], up, me_c)
    send(1, V.at[0, pl.ds(D + rows - S, S), :, body], V.at[0, pl.ds(D - S, S), :, body], down, me_c)
    send(2, V.at[0, inner, :, lo], RE, me_r, west)
    send(3, V.at[0, inner, :, hi], RW, me_r, east)

    for load in loads[1:]:
        load.wait()
    for r0, c0 in tiles:
        rsl, sl = pl.ds(r0, 8), pl.ds(c0, LANES)
        row_id = lax.broadcasted_iota(jnp.int32, (8, LANES), 0) + (me_r * rows + r0)
        col_id = lane + (me_c * own + c0)
        ec, lc = ecls[rsl, sl], lcls[rsl, sl]
        e = jnp.zeros((8, LANES), f32)
        l = jnp.zeros((8, LANES), f32)
        for k in range(table.shape[0]):
            e = jnp.where(ec == k, table[k], e)
            l = jnp.where(lc == k, table[k], l)
        at = pl.ds(CH + r0, 8)
        ELP[0, at, sl] = jnp.where(col_id < nc * own - 1, e, 0.0)
        ELP[1, at, sl] = jnp.where(row_id < nr * rows - 1, l, 0.0)
        ELP[2, at, sl] = PAD_G * via[rsl, sl].astype(f32)
    cinner = pl.ds(CH, rows)
    send(4, ELP.at[:, pl.ds(CH, 8), body], ELP.at[:, pl.ds(CH + rows, 8), body], up, me_c)
    send(5, ELP.at[:, pl.ds(CH + rows - 8, 8), body], ELP.at[:, pl.ds(CH - 8, 8), body], down, me_c)
    send(6, ELP.at[:, cinner, lo], CE, me_r, west)
    send(7, ELP.at[:, cinner, hi], CW, me_r, east)
    for n, (bottom, right) in enumerate(((0, 0), (0, 1), (1, 0), (1, 1))):
        sl = hi if right else lo
        x = jnp.zeros((8, LANES), f32)
        for j in range(D):
            i = (rows if bottom else D) + j
            x = jnp.where(lane >= 12 * j, pltpu.roll(V[0, i, :, sl], (12 * j + 10 * right) % LANES, 1), x)
        CS[n, 0] = x
        x = jnp.zeros((8, LANES), f32)
        for j in range(6):
            i = (rows if bottom else CH) + 8 * (j % 2)
            x = jnp.where(
                lane >= 16 * j, pltpu.roll(ELP[j // 2, pl.ds(i, 8), sl], (16 * j + 16 * right) % LANES, 1), x
            )
        CS[n, 1] = x
        send(8 + n, CS.at[n], CR.at[n], down if bottom else up, east if right else west)
    send(12, V.at[0, pl.ds(D + S, S), :, body], V.at[0, pl.ds(D + rows + S, S), :, body], up, me_c)
    send(13, V.at[0, pl.ds(rows, S), :, body], V.at[0, pl.ds(0, S), :, body], down, me_c)
    send(14, ELP.at[:, pl.ds(CH + 8, 8), body], ELP.at[:, pl.ds(CH + rows + 8, 8), body], up, me_c)
    send(15, ELP.at[:, pl.ds(rows, 8), body], ELP.at[:, pl.ds(0, 8), body], down, me_c)

    scale = 1.0 / SHIFT
    side = pl.ds(own, LANES)
    everywhere = pl.ds(0, width)

    def expand(first, count, sl, planes):
        for i in range(first, first + count):
            for p in planes:
                at = pl.ds(i + CH - D, 1)
                x = ELP[p, at, sl] * scale if p < 2 else CP[at, sl]
                (E, L, C)[p][i, :, sl] = jnp.broadcast_to(x, (8, sl.size))

    expand(D, rows, body, (0, 1))
    for n in range(12):
        copies[n].wait_recv()

    left = lane < LANES // 2

    def side_row(i, c):
        V[0, i, :, side] = jnp.where(left, RE[i - D], RW[i - D])
        return c

    lax.fori_loop(D, D + rows, side_row, 0, unroll=4)
    for bottom in range(2):
        a, b = 2 - 2 * bottom, 3 - 2 * bottom
        for j in range(D):
            i = (D + rows if bottom else 0) + j
            V[0, i, :, side] = jnp.where(
                left,
                pltpu.roll(CR[a, 0], (LANES - 12 * j) % LANES, 1),
                pltpu.roll(CR[b, 0], (LANES - 10 - 12 * j) % LANES, 1),
            )
        for j in range(6):
            at = pl.ds((CH + rows if bottom else 0) + 8 * (j % 2), 8)
            ELP[j // 2, at, side] = jnp.where(
                left,
                pltpu.roll(CR[a, 1], (LANES - 16 * j) % LANES, 1),
                pltpu.roll(CR[b, 1], (LANES - 16 - 16 * j) % LANES, 1),
            )
    for p in range(3):
        for r0 in range(0, rows, 8):
            at = pl.ds(r0, 8)
            ELP[p, pl.ds(CH + r0, 8), side] = jnp.where(left, CE[p, at], CW[p, at])

    def centre(first, count):
        at = pl.ds(first, count)
        e, l = ELP[0, at], ELP[1, at]
        around = (e + pltpu.roll(e, 1, 1)) + (l + pltpu.roll(l, 1, 0))
        CP[at] = (around + (ELP[2, at] + LEAK)) * scale - 1.0

    centre(CH - 8, rows + 16)
    expand(D - S, S, everywhere, (0, 1))
    expand(D + rows, S, everywhere, (0, 1))
    expand(D, rows, side, (0, 1))
    expand(D - S, rows + 2 * S, everywhere, (2,))

    def allsum(phase, tile, me, n, device, meanwhile):
        RB[phase, me] = tile
        for d in range(1, n):
            pltpu.make_async_remote_copy(
                src_ref=RB.at[phase, me], dst_ref=RB.at[phase, me],
                send_sem=rs.at[phase], recv_sem=rr.at[phase],
                device_id=device((me + d) % n), device_id_type=MESH,
            ).start()
        meanwhile()
        pending(phase, n).wait_recv()
        parts = [RB[phase, d] for d in range(n)]
        while len(parts) > 1:
            odd = parts[len(parts) // 2 * 2 :]
            parts = [parts[j] + parts[j + 1] for j in range(0, len(parts) - 1, 2)] + odd
        return parts[0]

    def pending(phase, n):
        some = RB.at[phase, pl.ds(0, n - 1)]
        return pltpu.make_async_remote_copy(
            src_ref=some, dst_ref=some, send_sem=rs.at[phase], recv_sem=rr.at[phase],
            device_id=(up, me_c), device_id_type=MESH,
        )

    def cast(first, count):
        for i in range(first, first + count):
            VB[i] = halves(jnp.concatenate([V[m, i] for m in range(S)], 0))

    def store(ref):
        def put(i, x):
            ref[i] = x

        return put

    def outer_rows():
        for n in range(12, 16):
            copies[n].wait_recv()
        centre(0, 16)
        centre(CH + rows, 16)
        expand(0, S + 1, everywhere, (0, 1, 2))
        expand(ext - S - 1, S + 1, everywhere, (0, 1, 2))
        for m in range(S - 1):
            stencil_rows(V.at[m], E, L, C, m + 1, S, store(V.at[m + 1]))
            stencil_rows(V.at[m], E, L, C, ext - S - 1 - m, S, store(V.at[m + 1]))

    def outer_cast(depth):
        cast(D - depth, depth)
        cast(D + rows, depth)

    for sweep in range(OUTER):

        def level(m, c):
            stencil_rows(V.at[m], E, L, C, D - S + 1, rows + 2 * S - 2, store(V.at[m + 1]))
            return c

        lax.fori_loop(0, S, level, 0)
        depth = S * (OUTER - 1 - sweep)
        tile = moments(V, VB, D, rows, own)
        tile = allsum(
            2 * sweep, tile, me_c, nc, lambda c: (me_r, c),
            outer_rows if sweep == 0 else lambda: outer_cast(depth + 1),
        )
        tile = allsum(
            2 * sweep + 1, tile, me_r, nr, lambda r: (r, me_c),
            (lambda: outer_cast(depth + 1)) if sweep == 0 else lambda: None,
        )
        if sweep == 0:
            for copy in copies:
                copy.wait_send()
        X = (X1, X2)[sweep]
        count = rows + 2 * depth + 2
        combine(VB, solve(tile), X, D - depth - 1, count, 11 if count % 11 == 0 else 17)

        def update(i, x):
            V[0, i] = V[0, i] - SHIFT * (x + X[i])

        stencil_rows(X, E, L, C, D - depth, rows + 2 * depth, update)

    for r0, c0 in tiles:
        rsl, sl = pl.ds(r0, 8), pl.ds(c0, LANES)
        at = pl.ds(D + r0, 8)
        xo[:, rsl, sl] = jnp.swapaxes(X1[at, :, sl] + X2[at, :, sl], 0, 1)
        ro[:, rsl, sl] = jnp.swapaxes(V[0, at, :, sl], 0, 1)
    for phase in range(2 * OUTER):
        pending(phase, (nc, nr)[phase % 2]).wait_send()


def local(right_side, east_class, lower_class, via_mask, class_conductance):
    nr, nc = lax.axis_size("rows"), lax.axis_size("cols")
    loads, rows, own = right_side.shape
    ext, width, crows = rows + 2 * D, own + LANES, rows + 2 * CH
    vmem = pl.BlockSpec(memory_space=pltpu.VMEM)
    field = pltpu.VMEM((ext, loads, width), f32)
    dma = pltpu.SemaphoreType.DMA
    return pl.pallas_call(
        functools.partial(kernel, nr, nc),
        out_shape=[jax.ShapeDtypeStruct(right_side.shape, f32)] * 2,
        in_specs=[pl.BlockSpec(memory_space=pltpu.HBM)] * 5,
        out_specs=[vmem] * 2,
        scratch_shapes=[
            pltpu.VMEM(right_side.shape, f32),
            pltpu.VMEM((rows, own), jnp.int32),
            pltpu.VMEM((rows, own), jnp.int32),
            pltpu.VMEM((rows, own), jnp.int32),
            pltpu.SMEM(class_conductance.shape, f32),
            pltpu.VMEM((S + 1, ext, loads, width), f32),
            pltpu.VMEM((ext, 2 * loads * S, width), bf16),
            field, field, field, field, field,
            pltpu.VMEM((3, crows, width), f32),
            pltpu.VMEM((crows, width), f32),
            pltpu.VMEM((rows, loads, LANES), f32),
            pltpu.VMEM((rows, loads, LANES), f32),
            pltpu.VMEM((3, rows, LANES), f32),
            pltpu.VMEM((3, rows, LANES), f32),
            pltpu.VMEM((4, 2, 8, LANES), f32),
            pltpu.VMEM((4, 2, 8, LANES), f32),
            pltpu.VMEM((2 * OUTER, max(nr, nc), 8, LANES), f32),
            dma((5,)),
            dma((16,)),
            dma((16,)),
            dma((2 * OUTER,)),
            dma((2 * OUTER,)),
        ],
        compiler_params=pltpu.CompilerParams(
            collective_id=0, has_side_effects=True, vmem_limit_bytes=40 * 2**20
        ),
    )(right_side, east_class, lower_class, via_mask, class_conductance)


def solution(mesh):
    return jax.shard_map(
        local,
        mesh=mesh,
        in_specs=(
            P(None, "rows", "cols"),
            P("rows", "cols"),
            P("rows", "cols"),
            P("rows", "cols"),
            P(),
        ),
        out_specs=(P(None, "rows", "cols"), P(None, "rows", "cols")),
        check_vma=False,
    )
```

time: 72.5 us -> 59 us (0.81)
  Pallas kernels: 65.8 us -> 52.3 us
    pallas_call x1, Pallas kernels: 65.8 us -> 52.3 us  [local(): pl.pallas_call(functools.partial(kernel, nr, nc), out_shape=[jax.ShapeDty...]
where the time goes in v1:
time: 59 us; the launch traced here: 58.7 us
  Pallas kernels  52.3 us (89%)
  local copies, waits for them, and re-layouts  5.79 us (10%)
  between operations  0.65 us (1%)
    pallas_call x1, Pallas kernels, local(): pl.pallas_call(functools.partial(kernel, nr, nc), out_shape=[jax.ShapeDty...  52.3 us
    unnamed x12, local copies, waits for them, and re-layouts  5.79 us

profile of v1, /device:TPU:1, one launch (start us, length us, event | category | flops | bytes accessed | tf_op | source)
XLA Modules:
  0.0 58.7 jit_solution(16579281640292441568)
XLA Ops:
  0.6 0.0 copy-start
  0.6 1.0 %copy-done = f32[8,32,512]{2,1,0:T(8,128)S(1)} copy-done((f32[8,32,512]{2,1,0:T(8,128)S(1)}, f32[8,32,512]{2,1,0:T(8,128)}, u32[]{:S(2)}) %copy-start) | copy-done | bytes 524312
  1.7 0.0 copy-start.1
  1.7 0.8 %copy-done.1 = s32[32,512]{1,0:T(8,128)S(1)} copy-done((s32[32,512]{1,0:T(8,128)S(1)}, s32[32,512]{1,0:T(8,128)}, u32[]{:S(2)}) %copy-start.1) | copy-done | bytes 65560
  2.5 0.0 copy-start.2
  2.5 0.8 %copy-done.2 = s32[32,512]{1,0:T(8,128)S(1)} copy-done((s32[32,512]{1,0:T(8,128)S(1)}, s32[32,512]{1,0:T(8,128)}, u32[]{:S(2)}) %copy-start.2) | copy-done | bytes 65560
  3.4 0.0 copy-start.3
  3.4 0.8 %copy-done.3 = s32[32,512]{1,0:T(8,128)S(1)} copy-done((s32[32,512]{1,0:T(8,128)S(1)}, s32[32,512]{1,0:T(8,128)}, u32[]{:S(2)}) %copy-start.3) | copy-done | bytes 65560
  4.2 0.0 copy-start.4
  4.2 0.7 %copy-done.4 = f32[16]{0:T(128)S(1)} copy-done((f32[16]{0:T(128)S(1)}, f32[16]{0:T(128)}, u32[]{:S(2)}) %copy-start.4) | copy-done | bytes 88
  4.8 52.3 %shard_map.68 = (f32[8,32,512]{2,1,0:T(8,128)S(1)}, f32[8,32,512]{2,1,0:T(8,128)S(1)}) custom-call(f32[8,32,512]{2,1,0:T(8,128)S(1)} %copy-done, s32[32,512]{1,0:T(8,128)S(1)} %copy-done.1, s32[32,512]{1,0:T(8,128)S(1)} %copy-done.2, s32[32,512]{1,0:T(8,128)S(1)} %copy-done.3, f32[16]{0:T(128)S(1)} %copy-done.4), custom_call_target="tpu_custom_call" | custom-call | tf_op jit(solution)/shard_map/pallas_call | solution.py:382
  57.1 0.8 %copy.9 = f32[8,32,512]{2,1,0:T(8,128)} copy(f32[8,32,512]{2,1,0:T(8,128)S(1)} %get-tuple-element.4) | data formatting | bytes 1048576
  57.9 0.8 %copy.10 = f32[8,32,512]{2,1,0:T(8,128)} copy(f32[8,32,512]{2,1,0:T(8,128)S(1)} %get-tuple-element.5) | data formatting | bytes 1048576
Async XLA Ops:
  0.6 1.0 %copy-start = (f32[8,32,512]{2,1,0:T(8,128)S(1)}, f32[8,32,512]{2,1,0:T(8,128)}, u32[]{:S(2)}) copy-start(f32[8,32,512]{2,1,0:T(8,128)} %rhs_in.1) | copy-start | bytes 1572868
  1.7 0.8 %copy-start.1 = (s32[32,512]{1,0:T(8,128)S(1)}, s32[32,512]{1,0:T(8,128)}, u32[]{:S(2)}) copy-start(s32[32,512]{1,0:T(8,128)} %ecls_in.1) | copy-start | bytes 196612
  2.5 0.8 %copy-start.2 = (s32[32,512]{1,0:T(8,128)S(1)}, s32[32,512]{1,0:T(8,128)}, u32[]{:S(2)}) copy-start(s32[32,512]{1,0:T(8,128)} %lcls_in.1) | copy-start | bytes 196612
  3.4 0.8 %copy-start.3 = (s32[32,512]{1,0:T(8,128)S(1)}, s32[32,512]{1,0:T(8,128)}, u32[]{:S(2)}) copy-start(s32[32,512]{1,0:T(8,128)} %via_in.1) | copy-start | bytes 196612
  4.2 0.7 %copy-start.4 = (f32[16]{0:T(128)S(1)}, f32[16]{0:T(128)}, u32[]{:S(2)}) copy-start(f32[16]{0:T(128)} %table_in.1) | copy-start | bytes 196

commit v2 on v1

--- a/solution.py
+++ b/solution.py
@@ -50,25 +50,31 @@
     return jnp.concatenate([high, low], 0)
 
 
-def moments(V, VB, first, rows, own, step=8):
+def products(V, VB, lines, own):
+    left, right = [], []
+    for i in lines:
+        b = [V[m, i] for m in range(S + 1)]
+        split = halves(jnp.concatenate(b[:S], 0))
+        VB[i] = split
+        left.append(split[:, :own])
+        right.append(
+            halves(jnp.concatenate([(b[m] + b[m + 1])[:, :own] for m in range(S)] + [b[0][:, :own]], 0))
+        )
+    return lax.dot_general(
+        jnp.concatenate(left, 1), jnp.concatenate(right, 1),
+        (((1,), (1,)), ((), ())), preferred_element_type=f32,
+    )
+
+
+def product_blocks(V, VB, first, blocks, step, own):
     def some(j, acc):
-        left, right = [], []
-        for q in range(step):
-            i = first + j * step + q
-            b = [V[m, i] for m in range(S + 1)]
-            split = halves(jnp.concatenate(b[:S], 0))
-            VB[i] = split
-            left.append(split[:, :own])
-            right.append(
-                halves(jnp.concatenate([(b[m] + b[m + 1])[:, :own] for m in range(S)] + [b[0][:, :own]], 0))
-            )
-        return acc + lax.dot_general(
-            jnp.concatenate(left, 1), jnp.concatenate(right, 1),
-            (((1,), (1,)), ((), ())), preferred_element_type=f32,
-        )
-
+        return acc + products(V, VB, [first + j * step + q for q in range(step)], own)
+
+    return lax.fori_loop(0, blocks, some, jnp.zeros((16 * S, 16 * (S + 1)), f32))
+
+
+def moments(acc):
     n, k = 8 * S, 8 * (S + 1)
-    acc = lax.fori_loop(0, rows // step, some, jnp.zeros((2 * n, 2 * k), f32))
     gram = (acc[:n, :k] + acc[n:, k:]) + (acc[:n, k:] + acc[n:, :k])
     gram = jnp.concatenate([gram, jnp.zeros((n, LANES - k), f32)], 1)
     block = lax.broadcasted_iota(jnp.int32, (8, LANES), 1) >> 3
@@ -133,7 +139,7 @@
 def kernel(
     nr, nc, rhs_in, ecls_in, lcls_in, via_in, table_in, xo, ro,
     rhs, ecls, lcls, via, table,
-    V, VB, E, L, C, X1, X2, ELP, CP, RE, RW, CE, CW, CS, CR, RB, ls, hs, hr, rs, rr,
+    V, VB, E, L, C, X1, X2, ELP, CP, PS, PR, CS, CR, RB, ls, hs, hr, rs, rr,
 ):
     rows, own = rhs.shape[1], rhs.shape[2]
     ext = rows + 2 * D
@@ -163,7 +169,7 @@
     for d in range(1, nr):
         greet((me_r + d) % nr, me_c)
 
-    copies = [None] * 16
+    copies = [None] * 14
 
     def send(n, src, dst, r, c):
         copies[n] = pltpu.make_async_remote_copy(
@@ -174,21 +180,8 @@
 
     lane = lax.broadcasted_iota(jnp.int32, (8, LANES), 1)
     tiles = [(8 * g, LANES * t) for g in range(rows // 8) for t in range(own // LANES)]
-    loads[0].wait()
-    for r0, c0 in tiles:
-        V[0, pl.ds(D + r0, 8), :, pl.ds(c0, LANES)] = jnp.swapaxes(
-            rhs[:, pl.ds(r0, 8), pl.ds(c0, LANES)], 0, 1
-        )
-
-    pl.semaphore_wait(barrier, nr + nc + 2)
-
     body = pl.ds(0, own)
-    lo, hi = pl.ds(0, LANES), pl.ds(own - LANES, LANES)
-    inner = pl.ds(D, rows)
-    send(0, V.at[0, pl.ds(D, S), :, body], V.at[0, pl.ds(D + rows, S), :, body], up, me_c)
-    send(1, V.at[0, pl.ds(D + rows - S, S), :, body], V.at[0, pl.ds(D - S, S), :, body], down, me_c)
-    send(2, V.at[0, inner, :, lo], RE, me_r, west)
-    send(3, V.at[0, inner, :, hi], RW, me_r, east)
+    ends = (pl.ds(0, LANES), pl.ds(own - LANES, LANES))
 
     for load in loads[1:]:
         load.wait()
@@ -206,34 +199,52 @@
         ELP[0, at, sl] = jnp.where(col_id < nc * own - 1, e, 0.0)
         ELP[1, at, sl] = jnp.where(row_id < nr * rows - 1, l, 0.0)
         ELP[2, at, sl] = PAD_G * via[rsl, sl].astype(f32)
-    cinner = pl.ds(CH, rows)
+    loads[0].wait()
+    for r0, c0 in tiles:
+        V[0, pl.ds(D + r0, 8), :, pl.ds(c0, LANES)] = jnp.swapaxes(
+            rhs[:, pl.ds(r0, 8), pl.ds(c0, LANES)], 0, 1
+        )
+
+    def pack(pieces, gap, skip):
+        x = jnp.zeros((8, LANES), f32)
+        for j, piece in enumerate(pieces):
+            x = jnp.where(lane >= gap * j, pltpu.roll(piece, (gap * j + skip) % LANES, 1), x)
+        return x
+
+    ntile = rows // 8
+    for right, sl in enumerate(ends):
+        for g in range(ntile):
+            PS[right, g] = pack([V[0, D + 8 * g + j, :, sl] for j in range(8)], 16, D * right)
+        planes = [ELP[p, pl.ds(CH + 8 * g, 8), sl] for p in range(3) for g in range(ntile)]
+        for q in range(0, len(planes), 8):
+            PS[right, ntile + q // 8] = pack(planes[q : q + 8], 16, 16 * right)
+        for bottom in range(2):
+            n = 2 * bottom + right
+            i, c = (rows, rows) if bottom else (D, CH)
+            CS[n, 0] = pack([V[0, i + j, :, sl] for j in range(D)], 12, D * right)
+            CS[n, 1] = pack(
+                [ELP[j // 2, pl.ds(c + 8 * (j % 2), 8), sl] for j in range(6)], 16, 16 * right
+            )
+
+    pl.semaphore_wait(barrier, nr + nc + 2)
+
+    send(0, V.at[0, pl.ds(D, S), :, body], V.at[0, pl.ds(D + rows, S), :, body], up, me_c)
+    send(1, V.at[0, pl.ds(D + rows - S, S), :, body], V.at[0, pl.ds(D - S, S), :, body], down, me_c)
+    send(2, PS.at[0], PR.at[0], me_r, west)
+    send(3, PS.at[1], PR.at[1], me_r, east)
     send(4, ELP.at[:, pl.ds(CH, 8), body], ELP.at[:, pl.ds(CH + rows, 8), body], up, me_c)
     send(5, ELP.at[:, pl.ds(CH + rows - 8, 8), body], ELP.at[:, pl.ds(CH - 8, 8), body], down, me_c)
-    send(6, ELP.at[:, cinner, lo], CE, me_r, west)
-    send(7, ELP.at[:, cinner, hi], CW, me_r, east)
-    for n, (bottom, right) in enumerate(((0, 0), (0, 1), (1, 0), (1, 1))):
-        sl = hi if right else lo
-        x = jnp.zeros((8, LANES), f32)
-        for j in range(D):
-            i = (rows if bottom else D) + j
-            x = jnp.where(lane >= 12 * j, pltpu.roll(V[0, i, :, sl], (12 * j + 10 * right) % LANES, 1), x)
-        CS[n, 0] = x
-        x = jnp.zeros((8, LANES), f32)
-        for j in range(6):
-            i = (rows if bottom else CH) + 8 * (j % 2)
-            x = jnp.where(
-                lane >= 16 * j, pltpu.roll(ELP[j // 2, pl.ds(i, 8), sl], (16 * j + 16 * right) % LANES, 1), x
-            )
-        CS[n, 1] = x
-        send(8 + n, CS.at[n], CR.at[n], down if bottom else up, east if right else west)
-    send(12, V.at[0, pl.ds(D + S, S), :, body], V.at[0, pl.ds(D + rows + S, S), :, body], up, me_c)
-    send(13, V.at[0, pl.ds(rows, S), :, body], V.at[0, pl.ds(0, S), :, body], down, me_c)
-    send(14, ELP.at[:, pl.ds(CH + 8, 8), body], ELP.at[:, pl.ds(CH + rows + 8, 8), body], up, me_c)
-    send(15, ELP.at[:, pl.ds(rows, 8), body], ELP.at[:, pl.ds(0, 8), body], down, me_c)
+    for n in range(4):
+        send(6 + n, CS.at[n], CR.at[n], down if n // 2 else up, east if n % 2 else west)
+    send(10, V.at[0, pl.ds(D + S, S), :, body], V.at[0, pl.ds(D + rows + S, S), :, body], up, me_c)
+    send(11, V.at[0, pl.ds(rows, S), :, body], V.at[0, pl.ds(0, S), :, body], down, me_c)
+    send(12, ELP.at[:, pl.ds(CH + 8, 8), body], ELP.at[:, pl.ds(CH + rows + 8, 8), body], up, me_c)
+    send(13, ELP.at[:, pl.ds(rows, 8), body], ELP.at[:, pl.ds(0, 8), body], down, me_c)
 
     scale = 1.0 / SHIFT
     side = pl.ds(own, LANES)
     everywhere = pl.ds(0, width)
+    left = lane < LANES // 2
 
     def expand(first, count, sl, planes):
         for i in range(first, first + count):
@@ -242,49 +253,69 @@
                 x = ELP[p, at, sl] * scale if p < 2 else CP[at, sl]
                 (E, L, C)[p][i, :, sl] = jnp.broadcast_to(x, (8, sl.size))
 
-    expand(D, rows, body, (0, 1))
-    for n in range(12):
-        copies[n].wait_recv()
-
-    left = lane < LANES // 2
-
-    def side_row(i, c):
-        V[0, i, :, side] = jnp.where(left, RE[i - D], RW[i - D])
-        return c
-
-    lax.fori_loop(D, D + rows, side_row, 0, unroll=4)
-    for bottom in range(2):
-        a, b = 2 - 2 * bottom, 3 - 2 * bottom
-        for j in range(D):
-            i = (D + rows if bottom else 0) + j
-            V[0, i, :, side] = jnp.where(
-                left,
-                pltpu.roll(CR[a, 0], (LANES - 12 * j) % LANES, 1),
-                pltpu.roll(CR[b, 0], (LANES - 10 - 12 * j) % LANES, 1),
-            )
-        for j in range(6):
-            at = pl.ds((CH + rows if bottom else 0) + 8 * (j % 2), 8)
-            ELP[j // 2, at, side] = jnp.where(
-                left,
-                pltpu.roll(CR[a, 1], (LANES - 16 * j) % LANES, 1),
-                pltpu.roll(CR[b, 1], (LANES - 16 - 16 * j) % LANES, 1),
-            )
-    for p in range(3):
-        for r0 in range(0, rows, 8):
-            at = pl.ds(r0, 8)
-            ELP[p, pl.ds(CH + r0, 8), side] = jnp.where(left, CE[p, at], CW[p, at])
-
     def centre(first, count):
         at = pl.ds(first, count)
         e, l = ELP[0, at], ELP[1, at]
         around = (e + pltpu.roll(e, 1, 1)) + (l + pltpu.roll(l, 1, 0))
         CP[at] = (around + (ELP[2, at] + LEAK)) * scale - 1.0
 
-    centre(CH - 8, rows + 16)
+    def unpack(east_piece, west_piece, shift, wide):
+        return jnp.where(
+            left,
+            pltpu.roll(east_piece, (LANES - shift) % LANES, 1),
+            pltpu.roll(west_piece, (LANES - wide - shift) % LANES, 1),
+        )
+
+    def store(ref):
+        def put(i, x):
+            ref[i] = x
+
+        return put
+
+    def rim(m, outside):
+        for first in (outside + m, ext - outside - m - S):
+            stencil_rows(V.at[m], E, L, C, first, S, store(V.at[m + 1]))
+
+    expand(D, rows, body, (0, 1))
+    for n in (2, 3):
+        copies[n].wait_recv()
+    for i in range(rows):
+        V[0, D + i, :, side] = unpack(PR[0, i // 8], PR[1, i // 8], 16 * (i % 8), D)
+    for j in range(3 * ntile):
+        q = ntile + j // 8
+        ELP[j // ntile, pl.ds(CH + 8 * (j % ntile), 8), side] = unpack(
+            PR[0, q], PR[1, q], 16 * (j % 8), 16
+        )
+    centre(CH, rows)
+    expand(D, rows, side, (0, 1))
+    expand(D + 1, rows - 1, everywhere, (2,))
+
+    def inner_level(m, c):
+        stencil_rows(V.at[m], E, L, C, D + 1, rows - 2, store(V.at[m + 1]))
+        return c
+
+    lax.fori_loop(0, S, inner_level, 0)
+    gram = product_blocks(V, VB, D + S, 2, (rows - 2 * S) // 2, own)
+
+    for n in (0, 1, 4, 5, 6, 7, 8, 9):
+        copies[n].wait_recv()
+    for bottom in range(2):
+        a, b = 2 - 2 * bottom, 3 - 2 * bottom
+        for j in range(D):
+            V[0, (D + rows) * bottom + j, :, side] = unpack(CR[a, 0], CR[b, 0], 12 * j, D)
+        for j in range(6):
+            at = pl.ds((CH + rows) * bottom + 8 * (j % 2), 8)
+            ELP[j // 2, at, side] = unpack(CR[a, 1], CR[b, 1], 16 * j, 16)
+    centre(CH - 8, 16)
+    centre(CH + rows - 8, 16)
     expand(D - S, S, everywhere, (0, 1))
-    expand(D + rows, S, everywhere, (0, 1))
-    expand(D, rows, side, (0, 1))
-    expand(D - S, rows + 2 * S, everywhere, (2,))
+    expand(D - S, S + 1, everywhere, (2,))
+    expand(D + rows, S, everywhere, (0, 1, 2))
+    for m in range(S):
+        rim(m, D - S + 1)
+    gram = gram + products(
+        V, VB, [D + j for j in range(S)] + [D + rows - S + j for j in range(S)], own
+    )
 
     def allsum(phase, tile, me, n, device, meanwhile):
         RB[phase, me] = tile
@@ -313,22 +344,15 @@
         for i in range(first, first + count):
             VB[i] = halves(jnp.concatenate([V[m, i] for m in range(S)], 0))
 
-    def store(ref):
-        def put(i, x):
-            ref[i] = x
-
-        return put
-
     def outer_rows():
-        for n in range(12, 16):
+        for n in range(10, 14):
             copies[n].wait_recv()
         centre(0, 16)
         centre(CH + rows, 16)
         expand(0, S + 1, everywhere, (0, 1, 2))
         expand(ext - S - 1, S + 1, everywhere, (0, 1, 2))
         for m in range(S - 1):
-            stencil_rows(V.at[m], E, L, C, m + 1, S, store(V.at[m + 1]))
-            stencil_rows(V.at[m], E, L, C, ext - S - 1 - m, S, store(V.at[m + 1]))
+            rim(m, 1)
 
     def outer_cast(depth):
         cast(D - depth, depth)
@@ -340,9 +364,11 @@
             stencil_rows(V.at[m], E, L, C, D - S + 1, rows + 2 * S - 2, store(V.at[m + 1]))
             return c
 
-        lax.fori_loop(0, S, level, 0)
+        if sweep:
+            lax.fori_loop(0, S, level, 0)
+            gram = product_blocks(V, VB, D, rows // 8, 8, own)
         depth = S * (OUTER - 1 - sweep)
-        tile = moments(V, VB, D, rows, own)
+        tile = moments(gram)
         tile = allsum(
             2 * sweep, tile, me_c, nc, lambda c: (me_r, c),
             outer_rows if sweep == 0 else lambda: outer_cast(depth + 1),
@@ -377,6 +403,7 @@
     loads, rows, own = right_side.shape
     ext, width, crows = rows + 2 * D, own + LANES, rows + 2 * CH
     vmem = pl.BlockSpec(memory_space=pltpu.VMEM)
+    packed = rows // 8 + -(-3 * (rows // 8) // 8)
     field = pltpu.VMEM((ext, loads, width), f32)
     dma = pltpu.SemaphoreType.DMA
     return pl.pallas_call(
@@ -395,23 +422,26 @@
             field, field, field, field, field,
             pltpu.VMEM((3, crows, width), f32),
             pltpu.VMEM((crows, width), f32),
-            pltpu.VMEM((rows, loads, LANES), f32),
-            pltpu.VMEM((rows, loads, LANES), f32),
-            pltpu.VMEM((3, rows, LANES), f32),
-            pltpu.VMEM((3, rows, LANES), f32),
+            pltpu.VMEM((2, packed, 8, LANES), f32),
+            pltpu.VMEM((2, packed, 8, LANES), f32),
             pltpu.VMEM((4, 2, 8, LANES), f32),
             pltpu.VMEM((4, 2, 8, LANES), f32),
             pltpu.VMEM((2 * OUTER, max(nr, nc), 8, LANES), f32),
             dma((5,)),
-            dma((16,)),
-            dma((16,)),
+            dma((14,)),
+            dma((14,)),
             dma((2 * OUTER,)),
             dma((2 * OUTER,)),
         ],
         compiler_params=pltpu.CompilerParams(
             collective_id=0, has_side_effects=True, vmem_limit_bytes=40 * 2**20
         ),
-    )(right_side, east_class, lower_class, via_mask, class_conductance)
+    )(
+        *(
+            pltpu.with_memory_space_constraint(x, pltpu.HBM)
+            for x in (right_side, east_class, lower_class, via_mask, class_conductance)
+        )
+    )
 
 
 def solution(mesh):

time: 59 us -> 51.1 us (0.87)
  local copies, waits for them, and re-layouts: 5.79 us -> 1.59 us
  Pallas kernels: 52.3 us -> 48.8 us
    unnamed x12 -> x2, local copies, waits for them, and re-layouts: 5.79 us -> 1.59 us
    pallas_call x1, Pallas kernels: 52.3 us -> 48.8 us  [local(): pl.pallas_call(functools.partial(kernel, nr, nc), out_shape=[jax.ShapeDty...]
where the time goes in v2:
time: 51.1 us; the launch traced here: 51 us
  Pallas kernels  48.8 us (95%)
  local copies, waits for them, and re-layouts  1.59 us (3%)
  between operations  0.64 us (1%)
    pallas_call x1, Pallas kernels, local(): pl.pallas_call(functools.partial(kernel, nr, nc), out_shape=[jax.ShapeDty...  48.8 us
    unnamed x2, local copies, waits for them, and re-layouts  1.59 us

profile of v2, /device:TPU:1, one launch (start us, length us, event | category | flops | bytes accessed | tf_op | source)
XLA Modules:
  0.0 51.0 jit_solution(1480942970498300343)
XLA Ops:
  0.6 48.8 %shard_map.68 = (f32[8,32,512]{2,1,0:T(8,128)S(1)}, f32[8,32,512]{2,1,0:T(8,128)S(1)}) custom-call(f32[8,32,512]{2,1,0:T(8,128)} %rhs_in.1, s32[32,512]{1,0:T(8,128)} %ecls_in.1, s32[32,512]{1,0:T(8,128)} %lcls_in.1, s32[32,512]{1,0:T(8,128)} %via_in.1, f32[16]{0:T(128)} %table_in.1), custom_call_target="tpu_custom_call" | custom-call | tf_op jit(solution)/shard_map/pallas_call | solution.py:409
  49.4 0.8 %copy.9 = f32[8,32,512]{2,1,0:T(8,128)} copy(f32[8,32,512]{2,1,0:T(8,128)S(1)} %get-tuple-element.4) | data formatting | bytes 1048576
  50.2 0.8 %copy.10 = f32[8,32,512]{2,1,0:T(8,128)} copy(f32[8,32,512]{2,1,0:T(8,128)S(1)} %get-tuple-element.5) | data formatting | bytes 1048576

commit v3 on v2

--- a/solution.py
+++ b/solution.py
@@ -36,29 +36,28 @@
         v = src[i]
         e = E[i]
         l = L[i]
-        put(
-            i,
-            (C[i] * v - e * pltpu.roll(v, width - 1, 1))
-            - (pltpu.roll(e * v, 1, 1) + (l * src[i + 1] + below)),
-        )
+        out = (C[i] * v - e * pltpu.roll(v, width - 1, 1)) - (
+            pltpu.roll(e * v, 1, 1) + (l * src[i + 1] + below)
+        )
+        put(i, v, out)
         below = l * v
 
 
-def halves(x):
-    high = x.astype(bf16)
-    low = (x - high.astype(f32)).astype(bf16)
-    return jnp.concatenate([high, low], 0)
-
-
-def products(V, VB, lines, own):
+def pair(x):
+    high = x.astype(bf16).astype(f32)
+    return jnp.concatenate([high, x - high], 0).astype(bf16)
+
+
+def stacked(planes, i, lanes):
+    return jnp.concatenate([plane[i][:, :lanes] for plane in planes], 0)
+
+
+def products(VB, WB, lines, own):
     left, right = [], []
     for i in lines:
-        b = [V[m, i] for m in range(S + 1)]
-        split = halves(jnp.concatenate(b[:S], 0))
-        VB[i] = split
-        left.append(split[:, :own])
+        left.append(stacked([VB.at[m] for m in range(S)], i - D, own))
         right.append(
-            halves(jnp.concatenate([(b[m] + b[m + 1])[:, :own] for m in range(S)] + [b[0][:, :own]], 0))
+            jnp.concatenate([stacked([WB.at[m] for m in range(S)], i, own), VB[0, i - D]], 0)
         )
     return lax.dot_general(
         jnp.concatenate(left, 1), jnp.concatenate(right, 1),
@@ -66,24 +65,25 @@
     )
 
 
-def product_blocks(V, VB, first, blocks, step, own):
+def product_blocks(VB, WB, first, blocks, step, own):
     def some(j, acc):
-        return acc + products(V, VB, [first + j * step + q for q in range(step)], own)
+        return acc + products(VB, WB, [first + j * step + q for q in range(step)], own)
 
     return lax.fori_loop(0, blocks, some, jnp.zeros((16 * S, 16 * (S + 1)), f32))
 
 
 def moments(acc):
-    n, k = 8 * S, 8 * (S + 1)
-    gram = (acc[:n, :k] + acc[n:, k:]) + (acc[:n, k:] + acc[n:, :k])
-    gram = jnp.concatenate([gram, jnp.zeros((n, LANES - k), f32)], 1)
     block = lax.broadcasted_iota(jnp.int32, (8, LANES), 1) >> 3
+    filler = jnp.zeros((8, LANES - 16 * (S + 1)), f32)
     out = jnp.zeros((8, LANES), f32)
     for m in range(S):
-        x = gram[8 * m : 8 * m + 8]
-        out = jnp.where((block >> 1) == m, x if m == 0 else pltpu.roll(x, 8 * m, 1), out)
-    for m in range(S):
-        x = pltpu.roll(gram[8 * m : 8 * m + 8], 32 + 8 * m, 1)
+        g = acc[16 * m : 16 * m + 8] + acc[16 * m + 8 : 16 * m + 16]
+        g = jnp.concatenate([g, filler], 1)
+        g = g + pltpu.roll(g, LANES - 8, 1)
+        out = jnp.where(block == 2 * m, g, out)
+        if m < S - 1:
+            out = jnp.where(block == 2 * m + 1, pltpu.roll(g, LANES - 8, 1), out)
+        x = g if m == 1 else pltpu.roll(g, (8 * m - 8) % LANES, 1)
         out = jnp.where(block == 9 + m, x, out)
     return out
 
@@ -118,19 +118,24 @@
     return T[S]
 
 
-def combine(VB, coefficients, X, first, rows, step):
-    lane = lax.broadcasted_iota(jnp.int32, (8, LANES), 1)
-    n = 8 * S
-    twice = jnp.where(lane < n, coefficients, pltpu.roll(coefficients, n, 1))
-    left = halves(twice)[:, : 2 * n]
-
+def weights(coefficients):
+    block = lax.broadcasted_iota(jnp.int32, (8, LANES), 1) >> 3
+    moved = [coefficients] + [pltpu.roll(coefficients, 8 * j, 1) for j in range(1, S + 1)]
+    x = jnp.zeros((8, LANES), f32)
+    for m in range(S):
+        x = jnp.where(block == 2 * m, moved[m], x)
+        x = jnp.where(block == 2 * m + 1, moved[m + 1], x)
+    return pair(x)[:, : 16 * S]
+
+
+def combine(left, right, first, rows, step, put):
     def some(j, c):
         for q in range(step):
             i = first + j * step + q
             out = lax.dot_general(
-                left, VB[i], (((1,), (0,)), ((), ())), preferred_element_type=f32
+                left, right(i), (((1,), (0,)), ((), ())), preferred_element_type=f32
             )
-            X[i] = out[:8] + out[8:]
+            put(i, out[:8] + out[8:])
         return c
 
     lax.fori_loop(0, rows // step, some, 0)
@@ -139,7 +144,7 @@
 def kernel(
     nr, nc, rhs_in, ecls_in, lcls_in, via_in, table_in, xo, ro,
     rhs, ecls, lcls, via, table,
-    V, VB, E, L, C, X1, X2, ELP, CP, PS, PR, CS, CR, RB, ls, hs, hr, rs, rr,
+    V, VBS, WB, E, L, C, X, ELP, CP, PS, PR, CS, CR, RB, ls, hs, hr, rs, rr,
 ):
     rows, own = rhs.shape[1], rhs.shape[2]
     ext = rows + 2 * D
@@ -183,27 +188,42 @@
     body = pl.ds(0, own)
     ends = (pl.ds(0, LANES), pl.ds(own - LANES, LANES))
 
+    def transpose_in(chosen):
+        for r0, c0 in chosen:
+            V[0, pl.ds(D + r0, 8), :, pl.ds(c0, LANES)] = jnp.swapaxes(
+                rhs[:, pl.ds(r0, 8), pl.ds(c0, LANES)], 0, 1
+            )
+
+    def look_up(chosen):
+        for r0, c0 in chosen:
+            rsl, sl = pl.ds(r0, 8), pl.ds(c0, LANES)
+            row_id = lax.broadcasted_iota(jnp.int32, (8, LANES), 0) + (me_r * rows + r0)
+            col_id = lane + (me_c * own + c0)
+            ec, lc = ecls[rsl, sl], lcls[rsl, sl]
+            e = jnp.zeros((8, LANES), f32)
+            l = jnp.zeros((8, LANES), f32)
+            for k in range(table.shape[0]):
+                e = jnp.where(ec == k, table[k], e)
+                l = jnp.where(lc == k, table[k], l)
+            at = pl.ds(CH + r0, 8)
+            ELP[0, at, sl] = jnp.where(col_id < nc * own - 1, e, 0.0)
+            ELP[1, at, sl] = jnp.where(row_id < nr * rows - 1, l, 0.0)
+            ELP[2, at, sl] = PAD_G * via[rsl, sl].astype(f32)
+
+    border = [at for at in tiles if at[0] in (0, rows - 8)]
+    others = [at for at in tiles if at not in border]
+    loads[0].wait()
+    transpose_in(border)
+    pl.semaphore_wait(barrier, nr + nc + 2)
+    send(0, V.at[0, pl.ds(D, S), :, body], V.at[0, pl.ds(D + rows, S), :, body], up, me_c)
+    send(1, V.at[0, pl.ds(D + rows - S, S), :, body], V.at[0, pl.ds(D - S, S), :, body], down, me_c)
     for load in loads[1:]:
         load.wait()
-    for r0, c0 in tiles:
-        rsl, sl = pl.ds(r0, 8), pl.ds(c0, LANES)
-        row_id = lax.broadcasted_iota(jnp.int32, (8, LANES), 0) + (me_r * rows + r0)
-        col_id = lane + (me_c * own + c0)
-        ec, lc = ecls[rsl, sl], lcls[rsl, sl]
-        e = jnp.zeros((8, LANES), f32)
-        l = jnp.zeros((8, LANES), f32)
-        for k in range(table.shape[0]):
-            e = jnp.where(ec == k, table[k], e)
-            l = jnp.where(lc == k, table[k], l)
-        at = pl.ds(CH + r0, 8)
-        ELP[0, at, sl] = jnp.where(col_id < nc * own - 1, e, 0.0)
-        ELP[1, at, sl] = jnp.where(row_id < nr * rows - 1, l, 0.0)
-        ELP[2, at, sl] = PAD_G * via[rsl, sl].astype(f32)
-    loads[0].wait()
-    for r0, c0 in tiles:
-        V[0, pl.ds(D + r0, 8), :, pl.ds(c0, LANES)] = jnp.swapaxes(
-            rhs[:, pl.ds(r0, 8), pl.ds(c0, LANES)], 0, 1
-        )
+    look_up(border)
+    send(4, ELP.at[:, pl.ds(CH, 8), body], ELP.at[:, pl.ds(CH + rows, 8), body], up, me_c)
+    send(5, ELP.at[:, pl.ds(CH + rows - 8, 8), body], ELP.at[:, pl.ds(CH - 8, 8), body], down, me_c)
+    transpose_in(others)
+    look_up(others)
 
     def pack(pieces, gap, skip):
         x = jnp.zeros((8, LANES), f32)
@@ -226,14 +246,8 @@
                 [ELP[j // 2, pl.ds(c + 8 * (j % 2), 8), sl] for j in range(6)], 16, 16 * right
             )
 
-    pl.semaphore_wait(barrier, nr + nc + 2)
-
-    send(0, V.at[0, pl.ds(D, S), :, body], V.at[0, pl.ds(D + rows, S), :, body], up, me_c)
-    send(1, V.at[0, pl.ds(D + rows - S, S), :, body], V.at[0, pl.ds(D - S, S), :, body], down, me_c)
     send(2, PS.at[0], PR.at[0], me_r, west)
     send(3, PS.at[1], PR.at[1], me_r, east)
-    send(4, ELP.at[:, pl.ds(CH, 8), body], ELP.at[:, pl.ds(CH + rows, 8), body], up, me_c)
-    send(5, ELP.at[:, pl.ds(CH + rows - 8, 8), body], ELP.at[:, pl.ds(CH - 8, 8), body], down, me_c)
     for n in range(4):
         send(6 + n, CS.at[n], CR.at[n], down if n // 2 else up, east if n % 2 else west)
     send(10, V.at[0, pl.ds(D + S, S), :, body], V.at[0, pl.ds(D + rows + S, S), :, body], up, me_c)
@@ -266,15 +280,19 @@
             pltpu.roll(west_piece, (LANES - wide - shift) % LANES, 1),
         )
 
-    def store(ref):
-        def put(i, x):
-            ref[i] = x
-
-        return put
-
-    def rim(m, outside):
+    def level(m, VB, first, count, widest):
+        def put(i, v, out):
+            V[m + 1, i] = out
+            if D <= i < D + rows:
+                VB[m, i - D] = pair(v[:, :own])
+            if widest <= i < ext - widest:
+                WB[m, i] = pair(v + out)
+
+        stencil_rows(V.at[m], E, L, C, first, count, put)
+
+    def rim(m, VB, outside):
         for first in (outside + m, ext - outside - m - S):
-            stencil_rows(V.at[m], E, L, C, first, S, store(V.at[m + 1]))
+            level(m, VB, first, S, D - S)
 
     expand(D, rows, body, (0, 1))
     for n in (2, 3):
@@ -290,12 +308,14 @@
     expand(D, rows, side, (0, 1))
     expand(D + 1, rows - 1, everywhere, (2,))
 
+    VB = VBS.at[0]
+
     def inner_level(m, c):
-        stencil_rows(V.at[m], E, L, C, D + 1, rows - 2, store(V.at[m + 1]))
+        level(m, VB, D + 1, rows - 2, D - S)
         return c
 
     lax.fori_loop(0, S, inner_level, 0)
-    gram = product_blocks(V, VB, D + S, 2, (rows - 2 * S) // 2, own)
+    gram = product_blocks(VB, WB, D + S, 2, (rows - 2 * S) // 2, own)
 
     for n in (0, 1, 4, 5, 6, 7, 8, 9):
         copies[n].wait_recv()
@@ -312,9 +332,9 @@
     expand(D - S, S + 1, everywhere, (2,))
     expand(D + rows, S, everywhere, (0, 1, 2))
     for m in range(S):
-        rim(m, D - S + 1)
+        rim(m, VB, D - S + 1)
     gram = gram + products(
-        V, VB, [D + j for j in range(S)] + [D + rows - S + j for j in range(S)], own
+        VB, WB, [D + j for j in range(S)] + [D + rows - S + j for j in range(S)], own
     )
 
     def allsum(phase, tile, me, n, device, meanwhile):
@@ -340,10 +360,6 @@
             device_id=(up, me_c), device_id_type=MESH,
         )
 
-    def cast(first, count):
-        for i in range(first, first + count):
-            VB[i] = halves(jnp.concatenate([V[m, i] for m in range(S)], 0))
-
     def outer_rows():
         for n in range(10, 14):
             copies[n].wait_recv()
@@ -351,49 +367,62 @@
         centre(CH + rows, 16)
         expand(0, S + 1, everywhere, (0, 1, 2))
         expand(ext - S - 1, S + 1, everywhere, (0, 1, 2))
-        for m in range(S - 1):
-            rim(m, 1)
-
-    def outer_cast(depth):
-        cast(D - depth, depth)
-        cast(D + rows, depth)
-
-    for sweep in range(OUTER):
-
-        def level(m, c):
-            stencil_rows(V.at[m], E, L, C, D - S + 1, rows + 2 * S - 2, store(V.at[m + 1]))
+        for m in range(S):
+            rim(m, VBS.at[0], 1)
+
+    def images(i):
+        return stacked([WB.at[m] for m in range(S)], i, width)
+
+    def bases(sweep, i):
+        return stacked([VBS.at[sweep, m] for m in range(S)], i - D, own)
+
+    def set_residual(i, x):
+        V[0, i] = V[0, i] - SHIFT * x
+
+    def set_solution(i, x):
+        X[i - D] = x
+
+    def reduce(tile, sweep, meanwhile):
+        tile = allsum(2 * sweep, tile, me_c, nc, lambda c: (me_r, c), meanwhile)
+        return allsum(2 * sweep + 1, tile, me_r, nr, lambda r: (r, me_c), lambda: None)
+
+    first_left = weights(solve(reduce(moments(gram), 0, outer_rows)))
+    for copy in copies:
+        copy.wait_send()
+    combine(first_left, images, D - S, rows + 2 * S, rows + 2 * S, set_residual)
+
+    VB = VBS.at[1]
+    half = S // 2
+    for start, stop in ((0, half), (half, S)):
+        lost = S - 1 - start
+
+        def some_level(m, c):
+            level(m, VB, D - lost, rows + 2 * lost, D)
             return c
 
-        if sweep:
-            lax.fori_loop(0, S, level, 0)
-            gram = product_blocks(V, VB, D, rows // 8, 8, own)
-        depth = S * (OUTER - 1 - sweep)
-        tile = moments(gram)
-        tile = allsum(
-            2 * sweep, tile, me_c, nc, lambda c: (me_r, c),
-            outer_rows if sweep == 0 else lambda: outer_cast(depth + 1),
-        )
-        tile = allsum(
-            2 * sweep + 1, tile, me_r, nr, lambda r: (r, me_c),
-            (lambda: outer_cast(depth + 1)) if sweep == 0 else lambda: None,
-        )
-        if sweep == 0:
-            for copy in copies:
-                copy.wait_send()
-        X = (X1, X2)[sweep]
-        count = rows + 2 * depth + 2
-        combine(VB, solve(tile), X, D - depth - 1, count, 11 if count % 11 == 0 else 17)
-
-        def update(i, x):
-            V[0, i] = V[0, i] - SHIFT * (x + X[i])
-
-        stencil_rows(X, E, L, C, D - depth, rows + 2 * depth, update)
-
+        lax.fori_loop(start, stop, some_level, 0)
+    gram = product_blocks(VB, WB, D, 2, rows // 2, own)
+    last_left = weights(
+        solve(
+            reduce(
+                moments(gram), 1,
+                lambda: combine(first_left, lambda i: bases(0, i), D, rows, 16, set_solution),
+            )
+        )
+    )
+
+    def finish(i, x):
+        X[i - D] = X[i - D] + x[:, :own]
+        V[0, i, :, body] = V[0, i, :, body] - SHIFT * x[:, own:]
+
+    combine(
+        last_left, lambda i: jnp.concatenate([bases(1, i), images(i)[:, :own]], 1),
+        D, rows, rows, finish,
+    )
     for r0, c0 in tiles:
         rsl, sl = pl.ds(r0, 8), pl.ds(c0, LANES)
-        at = pl.ds(D + r0, 8)
-        xo[:, rsl, sl] = jnp.swapaxes(X1[at, :, sl] + X2[at, :, sl], 0, 1)
-        ro[:, rsl, sl] = jnp.swapaxes(V[0, at, :, sl], 0, 1)
+        xo[:, rsl, sl] = jnp.swapaxes(X[rsl, :, sl], 0, 1)
+        ro[:, rsl, sl] = jnp.swapaxes(V[0, pl.ds(D + r0, 8), :, sl], 0, 1)
     for phase in range(2 * OUTER):
         pending(phase, (nc, nr)[phase % 2]).wait_send()
 
@@ -418,8 +447,10 @@
             pltpu.VMEM((rows, own), jnp.int32),
             pltpu.SMEM(class_conductance.shape, f32),
             pltpu.VMEM((S + 1, ext, loads, width), f32),
-            pltpu.VMEM((ext, 2 * loads * S, width), bf16),
-            field, field, field, field, field,
+            pltpu.VMEM((OUTER, S, rows, 2 * loads, own), bf16),
+            pltpu.VMEM((S, ext, 2 * loads, width), bf16),
+            field, field, field,
+            pltpu.VMEM((rows, loads, own), f32),
             pltpu.VMEM((3, crows, width), f32),
             pltpu.VMEM((crows, width), f32),
             pltpu.VMEM((2, packed, 8, LANES), f32),

time: 51.1 us -> 49 us (0.959)
  Pallas kernels: 48.8 us -> 46.7 us
    pallas_call x1, Pallas kernels: 48.8 us -> 46.7 us  [local(): pl.pallas_call(functools.partial(kernel, nr, nc), out_shape=[jax.ShapeDty...]
where the time goes in v3:
time: 49 us; the launch traced here: 48.9 us
  Pallas kernels  46.7 us (95%)
  local copies, waits for them, and re-layouts  1.59 us (3%)
  between operations  0.64 us (1%)
    pallas_call x1, Pallas kernels, local(): pl.pallas_call(functools.partial(kernel, nr, nc), out_shape=[jax.ShapeDty...  46.7 us
    unnamed x2, local copies, waits for them, and re-layouts  1.59 us

profile of v3, /device:TPU:1, one launch (start us, length us, event | category | flops | bytes accessed | tf_op | source)
XLA Modules:
  0.0 48.9 jit_solution(13909070946222302314)
XLA Ops:
  0.6 46.7 %shard_map.68 = (f32[8,32,512]{2,1,0:T(8,128)S(1)}, f32[8,32,512]{2,1,0:T(8,128)S(1)}) custom-call(f32[8,32,512]{2,1,0:T(8,128)} %rhs_in.1, s32[32,512]{1,0:T(8,128)} %ecls_in.1, s32[32,512]{1,0:T(8,128)} %lcls_in.1, s32[32,512]{1,0:T(8,128)} %via_in.1, f32[16]{0:T(128)} %table_in.1), custom_call_target="tpu_custom_call" | custom-call | tf_op jit(solution)/shard_map/pallas_call | solution.py:438
  47.3 0.8 %copy.9 = f32[8,32,512]{2,1,0:T(8,128)} copy(f32[8,32,512]{2,1,0:T(8,128)S(1)} %get-tuple-element.4) | data formatting | bytes 1048576
  48.1 0.8 %copy.10 = f32[8,32,512]{2,1,0:T(8,128)} copy(f32[8,32,512]{2,1,0:T(8,128)S(1)} %get-tuple-element.5) | data formatting | bytes 1048576

commit v4 on v3

--- a/solution.py
+++ b/solution.py
@@ -28,19 +28,23 @@
     return jnp.broadcast_to(x[row : row + 1, :], x.shape)
 
 
-def stencil_rows(src, E, L, C, first, count, put):
-    width = src.shape[-1]
-    below = L[first - 1] * src[first - 1]
+def whole(ref, i):
+    return ref[i]
+
+
+def stencil_rows(src, E, L, C, first, count, put, view=whole):
+    v = view(src, first)
+    width = v.shape[-1]
+    below = view(L, first - 1) * view(src, first - 1)
     for q in range(count):
         i = first + q
-        v = src[i]
-        e = E[i]
-        l = L[i]
-        out = (C[i] * v - e * pltpu.roll(v, width - 1, 1)) - (
-            pltpu.roll(e * v, 1, 1) + (l * src[i + 1] + below)
+        e, l, after = view(E, i), view(L, i), view(src, i + 1)
+        out = (view(C, i) * v - e * pltpu.roll(v, width - 1, 1)) - (
+            pltpu.roll(e * v, 1, 1) + (l * after + below)
         )
         put(i, v, out)
         below = l * v
+        v = after
 
 
 def pair(x):
@@ -48,16 +52,18 @@
     return jnp.concatenate([high, x - high], 0).astype(bf16)
 
 
-def stacked(planes, i, lanes):
-    return jnp.concatenate([plane[i][:, :lanes] for plane in planes], 0)
-
-
-def products(VB, WB, lines, own):
+def stacked(planes, i, pick):
+    return jnp.concatenate([pick(plane[i]) for plane in planes], 0)
+
+
+def products(VB, WB, lines, pick):
     left, right = [], []
     for i in lines:
-        left.append(stacked([VB.at[m] for m in range(S)], i - D, own))
+        left.append(stacked([VB.at[m] for m in range(S)], i - D, pick))
         right.append(
-            jnp.concatenate([stacked([WB.at[m] for m in range(S)], i, own), VB[0, i - D]], 0)
+            jnp.concatenate(
+                [stacked([WB.at[m] for m in range(S)], i, pick), pick(VB[0, i - D])], 0
+            )
         )
     return lax.dot_general(
         jnp.concatenate(left, 1), jnp.concatenate(right, 1),
@@ -65,9 +71,9 @@
     )
 
 
-def product_blocks(VB, WB, first, blocks, step, own):
+def product_blocks(VB, WB, first, blocks, step, pick):
     def some(j, acc):
-        return acc + products(VB, WB, [first + j * step + q for q in range(step)], own)
+        return acc + products(VB, WB, [first + j * step + q for q in range(step)], pick)
 
     return lax.fori_loop(0, blocks, some, jnp.zeros((16 * S, 16 * (S + 1)), f32))
 
@@ -144,7 +150,7 @@
 def kernel(
     nr, nc, rhs_in, ecls_in, lcls_in, via_in, table_in, xo, ro,
     rhs, ecls, lcls, via, table,
-    V, VBS, WB, E, L, C, X, ELP, CP, PS, PR, CS, CR, RB, ls, hs, hr, rs, rr,
+    V, VBS, WB, E, L, C, X, ELP, CP, PS, PR, CS, CR, KS, KR, KF, RB, ls, hs, hr, rs, rr,
 ):
     rows, own = rhs.shape[1], rhs.shape[2]
     ext = rows + 2 * D
@@ -154,27 +160,28 @@
     up, down = (me_r + nr - 1) % nr, (me_r + 1) % nr
     west, east = (me_c + nc - 1) % nc, (me_c + 1) % nc
 
+    barrier = pltpu.get_barrier_semaphore()
+
+    def greet(r, c):
+        pl.semaphore_signal(barrier, inc=1, device_id=(r, c), device_id_type=MESH)
+
+    for r, c in ((up, me_c), (down, me_c), (me_r, west), (me_r, east)):
+        greet(r, c)
+    for r in (up, down):
+        for c in (west, east):
+            greet(r, c)
     loads = []
     for j, (src, dst) in enumerate(
         ((rhs_in, rhs), (ecls_in, ecls), (lcls_in, lcls), (via_in, via), (table_in, table))
     ):
         loads.append(pltpu.make_async_copy(src, dst, ls.at[j]))
         loads[-1].start()
-
-    barrier = pltpu.get_barrier_semaphore()
-
-    def greet(r, c):
-        pl.semaphore_signal(barrier, inc=1, device_id=(r, c), device_id_type=MESH)
-
-    for r in (up, down):
-        for c in (west, east):
-            greet(r, c)
-    for d in range(1, nc):
+    for d in range(2, nc - 1):
         greet(me_r, (me_c + d) % nc)
-    for d in range(1, nr):
+    for d in range(2, nr - 1):
         greet((me_r + d) % nr, me_c)
 
-    copies = [None] * 14
+    copies = [None] * 20
 
     def send(n, src, dst, r, c):
         copies[n] = pltpu.make_async_remote_copy(
@@ -210,20 +217,11 @@
             ELP[1, at, sl] = jnp.where(row_id < nr * rows - 1, l, 0.0)
             ELP[2, at, sl] = PAD_G * via[rsl, sl].astype(f32)
 
-    border = [at for at in tiles if at[0] in (0, rows - 8)]
-    others = [at for at in tiles if at not in border]
-    loads[0].wait()
-    transpose_in(border)
-    pl.semaphore_wait(barrier, nr + nc + 2)
-    send(0, V.at[0, pl.ds(D, S), :, body], V.at[0, pl.ds(D + rows, S), :, body], up, me_c)
-    send(1, V.at[0, pl.ds(D + rows - S, S), :, body], V.at[0, pl.ds(D - S, S), :, body], down, me_c)
     for load in loads[1:]:
         load.wait()
-    look_up(border)
-    send(4, ELP.at[:, pl.ds(CH, 8), body], ELP.at[:, pl.ds(CH + rows, 8), body], up, me_c)
-    send(5, ELP.at[:, pl.ds(CH + rows - 8, 8), body], ELP.at[:, pl.ds(CH - 8, 8), body], down, me_c)
-    transpose_in(others)
-    look_up(others)
+    look_up(tiles)
+    loads[0].wait()
+    transpose_in(tiles)
 
     def pack(pieces, gap, skip):
         x = jnp.zeros((8, LANES), f32)
@@ -238,6 +236,22 @@
         planes = [ELP[p, pl.ds(CH + 8 * g, 8), sl] for p in range(3) for g in range(ntile)]
         for q in range(0, len(planes), 8):
             PS[right, ntile + q // 8] = pack(planes[q : q + 8], 16, 16 * right)
+
+    pl.semaphore_wait(barrier, nr + nc + 2)
+    send(0, V.at[0, pl.ds(D, S), :, body], V.at[0, pl.ds(D + rows, S), :, body], up, me_c)
+    send(1, V.at[0, pl.ds(D + rows - S, S), :, body], V.at[0, pl.ds(D - S, S), :, body], down, me_c)
+    first8, last8 = pl.ds(CH, 8), pl.ds(CH + rows - 8, 8)
+    after8, before8 = pl.ds(CH + rows, 8), pl.ds(CH - 8, 8)
+    top = lax.broadcasted_iota(jnp.int32, (8, own), 0) < 4
+    KS[0] = jnp.where(top, ELP[0, first8, body], pltpu.roll(ELP[2, first8, body], 4, 0))
+    KS[1] = jnp.where(top, pltpu.roll(ELP[2, last8, body], 4, 0), ELP[0, last8, body])
+    send(14, KS.at[0], KR.at[0], up, me_c)
+    send(15, KS.at[1], KR.at[1], down, me_c)
+    send(4, ELP.at[1, first8, body], ELP.at[1, after8, body], up, me_c)
+    send(5, ELP.at[1, last8, body], ELP.at[1, before8, body], down, me_c)
+    send(2, PS.at[0], PR.at[0], me_r, west)
+    send(3, PS.at[1], PR.at[1], me_r, east)
+    for right, sl in enumerate(ends):
         for bottom in range(2):
             n = 2 * bottom + right
             i, c = (rows, rows) if bottom else (D, CH)
@@ -245,15 +259,15 @@
             CS[n, 1] = pack(
                 [ELP[j // 2, pl.ds(c + 8 * (j % 2), 8), sl] for j in range(6)], 16, 16 * right
             )
-
-    send(2, PS.at[0], PR.at[0], me_r, west)
-    send(3, PS.at[1], PR.at[1], me_r, east)
     for n in range(4):
         send(6 + n, CS.at[n], CR.at[n], down if n // 2 else up, east if n % 2 else west)
     send(10, V.at[0, pl.ds(D + S, S), :, body], V.at[0, pl.ds(D + rows + S, S), :, body], up, me_c)
     send(11, V.at[0, pl.ds(rows, S), :, body], V.at[0, pl.ds(0, S), :, body], down, me_c)
     send(12, ELP.at[:, pl.ds(CH + 8, 8), body], ELP.at[:, pl.ds(CH + rows + 8, 8), body], up, me_c)
     send(13, ELP.at[:, pl.ds(rows, 8), body], ELP.at[:, pl.ds(0, 8), body], down, me_c)
+    for j, p in enumerate((0, 2)):
+        send(16 + j, ELP.at[p, first8, body], KF.at[0, j], up, me_c)
+        send(18 + j, ELP.at[p, last8, body], KF.at[1, j], down, me_c)
 
     scale = 1.0 / SHIFT
     side = pl.ds(own, LANES)
@@ -267,11 +281,11 @@
                 x = ELP[p, at, sl] * scale if p < 2 else CP[at, sl]
                 (E, L, C)[p][i, :, sl] = jnp.broadcast_to(x, (8, sl.size))
 
-    def centre(first, count):
+    def centre(first, count, sl):
         at = pl.ds(first, count)
-        e, l = ELP[0, at], ELP[1, at]
+        e, l = ELP[0, at, sl], ELP[1, at, sl]
         around = (e + pltpu.roll(e, 1, 1)) + (l + pltpu.roll(l, 1, 0))
-        CP[at] = (around + (ELP[2, at] + LEAK)) * scale - 1.0
+        CP[at, sl] = (around + (ELP[2, at, sl] + LEAK)) * scale - 1.0
 
     def unpack(east_piece, west_piece, shift, wide):
         return jnp.where(
@@ -295,6 +309,62 @@
             level(m, VB, first, S, D - S)
 
     expand(D, rows, body, (0, 1))
+    centre(CH, rows, body)
+    expand(D + 1, rows - 1, pl.ds(LANES, own - LANES), (2,))
+    VB = VBS.at[0]
+    half = S // 2
+    mid = slice(LANES, own - LANES)
+    spare = slice(own - LANES, own)
+
+    def owned(x):
+        return x[:, :own]
+
+    def middle(x):
+        return x[:, mid]
+
+    def outer(x):
+        return jnp.concatenate([x[:, :LANES], x[:, spare]], 1)
+
+    def inner_levels(one):
+        for start, stop in ((0, half), (half, S)):
+
+            def some_level(m, c):
+                one(m, D + 1 + start, rows - 2 - 2 * start)
+                return c
+
+            lax.fori_loop(start, stop, some_level, 0)
+
+    def middle_level(m, first, count):
+        def put(i, v, out):
+            V[m + 1, i, :, body] = out
+            VB[m, i - D, :, mid] = pair(middle(v))
+            WB[m, i, :, mid] = pair(middle(v) + middle(out))
+
+        stencil_rows(V.at[m], E, L, C, first, count, put, lambda ref, i: ref[i, :, body])
+
+    def outer_level(m, first, count):
+        def view(ref, i):
+            return jnp.concatenate([ref[i, :, own - LANES :], ref[i, :, :LANES]], 1)
+
+        def put(i, v, out):
+            last = jnp.where(left, V[m + 1, i, :, spare], out[:, :LANES])
+            start = jnp.where(left, out[:, 2 * LANES :], V[m + 1, i, :, :LANES])
+            V[m + 1, i, :, own - LANES :] = jnp.concatenate([last, out[:, LANES : 2 * LANES]], 1)
+            V[m + 1, i, :, :LANES] = start
+            basis = pair(v)
+            VB[m, i - D, :, spare] = basis[:, :LANES]
+            VB[m, i - D, :, :LANES] = basis[:, 2 * LANES :]
+            image = pair(v + jnp.concatenate([last, out[:, LANES : 2 * LANES], start], 1))
+            WB[m, i, :, own - LANES :] = image[:, : 2 * LANES]
+            WB[m, i, :, :LANES] = image[:, 2 * LANES :]
+
+        stencil_rows(V.at[m], E, L, C, first, count, put, view)
+
+    expand(D + 1, rows - 1, ends[0], (2,))
+    inner_levels(middle_level)
+    inside = (D + S, 2, (rows - 2 * S) // 2)
+    gram = product_blocks(VB, WB, *inside, middle)
+
     for n in (2, 3):
         copies[n].wait_recv()
     for i in range(rows):
@@ -304,21 +374,19 @@
         ELP[j // ntile, pl.ds(CH + 8 * (j % ntile), 8), side] = unpack(
             PR[0, q], PR[1, q], 16 * (j % 8), 16
         )
-    centre(CH, rows)
+    centre(CH, rows, everywhere)
     expand(D, rows, side, (0, 1))
-    expand(D + 1, rows - 1, everywhere, (2,))
-
-    VB = VBS.at[0]
-
-    def inner_level(m, c):
-        level(m, VB, D + 1, rows - 2, D - S)
-        return c
-
-    lax.fori_loop(0, S, inner_level, 0)
-    gram = product_blocks(VB, WB, D + S, 2, (rows - 2 * S) // 2, own)
-
-    for n in (0, 1, 4, 5, 6, 7, 8, 9):
+    expand(D + 1, rows - 1, side, (2,))
+    expand(D + 1, rows - 1, ends[0], (2,))
+
+    inner_levels(outer_level)
+    gram = gram + product_blocks(VB, WB, *inside, outer)
+
+    for n in (0, 1, 4, 5, 6, 7, 8, 9, 14, 15):
         copies[n].wait_recv()
+    for n, at in enumerate((after8, before8)):
+        ELP[0, at, body] = KR[n]
+        ELP[2, at, body] = pltpu.roll(KR[n], 4, 0)
     for bottom in range(2):
         a, b = 2 - 2 * bottom, 3 - 2 * bottom
         for j in range(D):
@@ -326,15 +394,15 @@
         for j in range(6):
             at = pl.ds((CH + rows) * bottom + 8 * (j % 2), 8)
             ELP[j // 2, at, side] = unpack(CR[a, 1], CR[b, 1], 16 * j, 16)
-    centre(CH - 8, 16)
-    centre(CH + rows - 8, 16)
+    centre(CH - 8, 16, everywhere)
+    centre(CH + rows - 8, 16, everywhere)
     expand(D - S, S, everywhere, (0, 1))
     expand(D - S, S + 1, everywhere, (2,))
     expand(D + rows, S, everywhere, (0, 1, 2))
     for m in range(S):
         rim(m, VB, D - S + 1)
     gram = gram + products(
-        VB, WB, [D + j for j in range(S)] + [D + rows - S + j for j in range(S)], own
+        VB, WB, [D + j for j in range(S)] + [D + rows - S + j for j in range(S)], owned
     )
 
     def allsum(phase, tile, me, n, device, meanwhile):
@@ -361,20 +429,23 @@
         )
 
     def outer_rows():
-        for n in range(10, 14):
+        for n in (10, 11, 12, 13, 16, 17, 18, 19):
             copies[n].wait_recv()
-        centre(0, 16)
-        centre(CH + rows, 16)
+        for n, at in enumerate((after8, before8)):
+            ELP[0, at, body] = KF[n, 0]
+            ELP[2, at, body] = KF[n, 1]
+        centre(0, 16, everywhere)
+        centre(CH + rows, 16, everywhere)
         expand(0, S + 1, everywhere, (0, 1, 2))
         expand(ext - S - 1, S + 1, everywhere, (0, 1, 2))
         for m in range(S):
             rim(m, VBS.at[0], 1)
 
     def images(i):
-        return stacked([WB.at[m] for m in range(S)], i, width)
+        return stacked([WB.at[m] for m in range(S)], i, lambda x: x)
 
     def bases(sweep, i):
-        return stacked([VBS.at[sweep, m] for m in range(S)], i - D, own)
+        return stacked([VBS.at[sweep, m] for m in range(S)], i - D, lambda x: x)
 
     def set_residual(i, x):
         V[0, i] = V[0, i] - SHIFT * x
@@ -392,7 +463,6 @@
     combine(first_left, images, D - S, rows + 2 * S, rows + 2 * S, set_residual)
 
     VB = VBS.at[1]
-    half = S // 2
     for start, stop in ((0, half), (half, S)):
         lost = S - 1 - start
 
@@ -401,7 +471,7 @@
             return c
 
         lax.fori_loop(start, stop, some_level, 0)
-    gram = product_blocks(VB, WB, D, 2, rows // 2, own)
+    gram = product_blocks(VB, WB, D, 2, rows // 2, owned)
     last_left = weights(
         solve(
             reduce(
@@ -457,10 +527,13 @@
             pltpu.VMEM((2, packed, 8, LANES), f32),
             pltpu.VMEM((4, 2, 8, LANES), f32),
             pltpu.VMEM((4, 2, 8, LANES), f32),
+            pltpu.VMEM((2, 8, own), f32),
+            pltpu.VMEM((2, 8, own), f32),
+            pltpu.VMEM((2, 2, 8, own), f32),
             pltpu.VMEM((2 * OUTER, max(nr, nc), 8, LANES), f32),
             dma((5,)),
-            dma((14,)),
-            dma((14,)),
+            dma((20,)),
+            dma((20,)),
             dma((2 * OUTER,)),
             dma((2 * OUTER,)),
         ],

time: 49 us -> 48.7 us (level)
  no operation moved by 1% of the time
where the time goes in v4:
time: 48.7 us; the launch traced here: 48.6 us
  Pallas kernels  46.4 us (95%)
  local copies, waits for them, and re-layouts  1.59 us (3%)
  between operations  0.64 us (1%)
    pallas_call x1, Pallas kernels, local(): pl.pallas_call(functools.partial(kernel, nr, nc), out_shape=[jax.ShapeDty...  46.4 us
    unnamed x2, local copies, waits for them, and re-layouts  1.59 us

profile of v4, /device:TPU:1, one launch (start us, length us, event | category | flops | bytes accessed | tf_op | source)
XLA Modules:
  0.0 48.6 jit_solution(14004587685408287470)
XLA Ops:
  0.6 46.4 %shard_map.68 = (f32[8,32,512]{2,1,0:T(8,128)S(1)}, f32[8,32,512]{2,1,0:T(8,128)S(1)}) custom-call(f32[8,32,512]{2,1,0:T(8,128)} %rhs_in.1, s32[32,512]{1,0:T(8,128)} %ecls_in.1, s32[32,512]{1,0:T(8,128)} %lcls_in.1, s32[32,512]{1,0:T(8,128)} %via_in.1, f32[16]{0:T(128)} %table_in.1), custom_call_target="tpu_custom_call" | custom-call | tf_op jit(solution)/shard_map/pallas_call | solution.py:508
  47.0 0.8 %copy.9 = f32[8,32,512]{2,1,0:T(8,128)} copy(f32[8,32,512]{2,1,0:T(8,128)S(1)} %get-tuple-element.4) | data formatting | bytes 1048576
  47.8 0.8 %copy.10 = f32[8,32,512]{2,1,0:T(8,128)} copy(f32[8,32,512]{2,1,0:T(8,128)S(1)} %get-tuple-element.5) | data formatting | bytes 1048576
